TPU v7x, 32 devices: a whole 2x2x4 slice. The times are simulated.
32 devices in a mesh: expert: 4 (over y, x), fsdp: 8 (over z, core).
Axes of the slice: x: 2, y: 2, z: 4, core: 2. Of those that a mesh axis runs over, the one named last changes fastest.
Arguments:
- tokens: bfloat16 [16384, 768], P(('expert', 'fsdp')), may hold values from -6 to 6
- past_logits: float32 [16384, 8], P(('expert', 'fsdp')), may hold values from -3 to 3
- routes: int32 [16384, 2], P(('expert', 'fsdp')), may hold values from 0 to 7, all different within a row; in each aligned block of 512 rows (0 to 511, 512 to 1023, ...) at most 128 rows name the same one
- lengths: int32 [4, 4], P('expert'), may hold values from 1 to 3840, 4096 in all within a row
- projector: bfloat16 [768, 2304], P('fsdp'), may hold values from -0.21875 to 0.21875
- collector: bfloat16 [768, 768], P('fsdp'), may hold values from -1.75 to 1.75
- router: bfloat16 [768, 8], P('fsdp'), may hold values from -0.109375 to 0.109375
- blender: bfloat16 [768, 4], P('fsdp'), may hold values from -0.21875 to 0.21875
- constants: bfloat16 [768, 2], P('fsdp'), may hold values from -5 to 5
- first_gain: bfloat16 [768], P('fsdp'), may hold values from 0.5 to 1.5
- second_gain: bfloat16 [768], P('fsdp'), may hold values from 0.5 to 1.5
- carryover: float32 [8, 8], replicated, may hold values from -2 to 2
- gating: bfloat16 [4, 768, 2048], P('expert', 'fsdp'), may hold values from -0.21875 to 0.21875
- upward: bfloat16 [4, 768, 2048], P('expert', 'fsdp'), may hold values from -0.21875 to 0.21875
- downward: bfloat16 [4, 768, 2048], P('expert', 'fsdp'), may hold values from -0.25 to 0.25
- cotangent: bfloat16 [16384, 768], P(('expert', 'fsdp')), may hold values from -6 to 6
Outputs:
- layer_output: bfloat16 [16384, 768], P(('expert', 'fsdp'))
- gradient_tokens: bfloat16 [16384, 768], P(('expert', 'fsdp'))
- gradient_logits: float32 [16384, 8], P(('expert', 'fsdp'))
- gradient_projector: float32 [768, 2304], P('fsdp')
- gradient_collector: float32 [768, 768], P('fsdp')
- gradient_router: float32 [768, 8], P('fsdp')
- gradient_blender: float32 [768, 4], P('fsdp')
- gradient_constants: float32 [768, 2], P('fsdp')
- gradient_first: float32 [768], P('fsdp')
- gradient_second: float32 [768], P('fsdp')
- gradient_carryover: float32 [8, 8], replicated
- gradient_gating: float32 [4, 768, 2048], P('expert', 'fsdp')
- gradient_upward: float32 [4, 768, 2048], P('expert', 'fsdp')
- gradient_downward: float32 [4, 768, 2048], P('expert', 'fsdp')
Inputs may be any that keep to these rules, and one draw needn't show every extreme that they name: `routes`: each row names two different experts: 0 to 3 are feed-forward experts, 4 the zero expert, 5 the copy expert, 6 and 7 the constant experts. Among the 512 rows of one device no expert is named more than 128 times, and in every draw some expert is named exactly 128 times among the rows of some device. Each row holds the lengths of the 4 documents packed in order into one sequence; they sum to 4096, and the longest is exactly 3840.
All inputs are finite; a program needn't handle non-finite values.
Results may differ from a plain program's by a relative error of at most 0.02.
Values may be sent and summed in bfloat16 or wider, within the bound.
No kernel may reach another device: no remote copies, remote signals or barrier semaphores. Data moves between devices by JAX's collectives and lax.ppermute only.
A program may use at most 256 MiB of HBM per device.

v0:
```python
import math

import jax
import jax.numpy as jnp
from jax import lax
from jax.sharding import PartitionSpec as P

D = 768
H = 12
HD = 64
FF = 2048
WINDOW = 1024
CAP = 128
HOPS = 2


epsilon = 1e-06
rope_base = 10000.0
masked_score = -1e30
contract_rows = (((0,), (0,)), ((), ()))
contract_cols = (((1,), (1,)), ((), ()))


def shifted(array, axis, by):
    size = lax.axis_size(axis)
    pairs = [(i, i + by) for i in range(size) if 0 <= i + by < size]
    return lax.ppermute(array, axis, pairs)


def norm_scale(values):
    return lax.rsqrt(jnp.mean(values * values, axis=-1, keepdims=True) + epsilon)


def softmax_rows(values):
    row_max = jnp.max(values, axis=-1, keepdims=True)
    exponent = jnp.exp(values - row_max)
    return exponent / jnp.sum(exponent, axis=-1, keepdims=True)


def rope_tables(positions, head_size):
    half_size = head_size // 2
    freq_index = jnp.arange(half_size).astype(jnp.float32)
    inverse = jnp.exp(freq_index * (-2.0 * math.log(rope_base) / head_size))
    angles = positions[:, None] * inverse[None, :]
    return (jnp.cos(angles)[:, None, :], jnp.sin(angles)[:, None, :])


def rotate(values, cosine_table, sine_table):
    half_size = values.shape[-1] // 2
    lower_half = values[..., :half_size]
    upper_half = values[..., half_size:]
    return jnp.concatenate(
        [
            lower_half * cosine_table - upper_half * sine_table,
            lower_half * sine_table + upper_half * cosine_table,
        ],
        axis=-1,
    )


def rotate_back(values, cosine_table, sine_table):
    half_size = values.shape[-1] // 2
    lower_half = values[..., :half_size]
    upper_half = values[..., half_size:]
    return jnp.concatenate(
        [
            lower_half * cosine_table + upper_half * sine_table,
            upper_half * cosine_table - lower_half * sine_table,
        ],
        axis=-1,
    )


def document_number(lengths_row, positions):
    bounds = jnp.cumsum(lengths_row)
    return jnp.sum((positions[:, None] >= bounds[None, :]).astype(jnp.int32), axis=1)


def allowed_keys(query_pos, query_docs, key_pos, key_docs, key_valid):
    distance = query_pos[:, None] - key_pos[None, :]
    inside = (distance >= 0) & (distance < WINDOW)
    return inside & (query_docs[:, None] == key_docs[None, :]) & key_valid[None, :]


def expert_forward(rows_in, gating_use, upward_use, downward_use):
    flat_rows = rows_in.reshape(-1, rows_in.shape[-1])
    gate_pre = jnp.dot(flat_rows, gating_use, preferred_element_type=jnp.float32)
    up_pre = jnp.dot(flat_rows, upward_use, preferred_element_type=jnp.float32)
    hidden = (jax.nn.silu(gate_pre) * up_pre).astype(jnp.bfloat16)
    answer = lax.dot_general(
        hidden, downward_use, contract_cols, preferred_element_type=jnp.float32
    )
    return answer.astype(jnp.bfloat16).reshape(rows_in.shape)


def local(
    tokens,
    past_logits,
    routes,
    lengths,
    projector,
    collector,
    router,
    blender,
    constants,
    first_gain,
    second_gain,
    carryover,
    gating,
    upward,
    downward,
    cotangent,
):
    tok_count = tokens.shape[0]
    expert_count = lax.axis_size("expert")
    shard_index = lax.axis_index("fsdp")
    highest = lax.Precision.HIGHEST
    shared = (
        lax.all_gather(projector, "fsdp", axis=0, tiled=True),
        lax.all_gather(collector, "fsdp", axis=0, tiled=True),
        lax.all_gather(router, "fsdp", axis=0, tiled=True),
        lax.all_gather(blender, "fsdp", axis=0, tiled=True),
        lax.all_gather(constants, "fsdp", axis=0, tiled=True),
        lax.all_gather(first_gain, "fsdp", axis=0, tiled=True),
        lax.all_gather(second_gain, "fsdp", axis=0, tiled=True),
    )
    projector_all, collector_all, router_all, blender_all, constants_all, first_all, second_all = (
        shared
    )
    router_wide = router_all.astype(jnp.float32)
    blender_wide = blender_all.astype(jnp.float32)
    constants_wide = constants_all.astype(jnp.float32)
    first_wide = first_all.astype(jnp.float32)
    second_wide = second_all.astype(jnp.float32)
    fetched = (
        lax.all_gather(gating, "fsdp", axis=1, tiled=True),
        lax.all_gather(upward, "fsdp", axis=1, tiled=True),
        lax.all_gather(downward, "fsdp", axis=1, tiled=True),
    )
    gating_all, upward_all, downward_all = (fetched[0][0], fetched[1][0], fetched[2][0])
    tokens_wide = tokens.astype(jnp.float32)
    first_scale = norm_scale(tokens_wide)
    normed = (tokens_wide * first_scale * first_wide).astype(jnp.bfloat16)
    projected = jnp.dot(normed, projector_all, preferred_element_type=jnp.float32).reshape(
        tok_count, 3, H, HD
    )
    positions = shard_index * tok_count + jnp.arange(tok_count, dtype=jnp.int32)
    cosine_table, sine_table = rope_tables(positions.astype(jnp.float32), HD)
    query_scale = 1.0 / math.sqrt(HD)
    queries = (rotate(projected[:, 0], cosine_table, sine_table) * query_scale).astype(jnp.bfloat16)
    keys_low = rotate(projected[:, 1], cosine_table, sine_table).astype(jnp.bfloat16)
    values_low = projected[:, 2].astype(jnp.bfloat16)
    key_parts = []
    value_parts = []
    for hop_count in range(HOPS, 0, -1):
        key_prev, value_prev = shifted(
            (keys_low.reshape(tok_count, D), values_low.reshape(tok_count, D)), "fsdp", hop_count
        )
        key_parts.append(key_prev)
        value_parts.append(value_prev)
    key_all = jnp.concatenate(key_parts + [keys_low.reshape(tok_count, D)], axis=0).reshape(
        -1, H, HD
    )
    value_all = jnp.concatenate(value_parts + [values_low.reshape(tok_count, D)], axis=0).reshape(
        -1, H, HD
    )
    span_rows = (HOPS + 1) * tok_count
    key_positions = (shard_index - HOPS) * tok_count + jnp.arange(span_rows, dtype=jnp.int32)
    query_docs = document_number(lengths[0], positions)
    key_docs = document_number(lengths[0], key_positions)
    key_valid = key_positions >= 0
    block_rows = min(512, tok_count)
    key_span = block_rows + WINDOW
    block_starts = list(range(0, tok_count, block_rows))

    def block_view(block_start):
        key_start = HOPS * tok_count + block_start - WINDOW
        allowed = allowed_keys(positions, query_docs, key_positions, key_docs, key_valid)
        return (key_start, allowed)

    attended_parts = []
    log_totals = []
    for block_start in block_starts:
        key_start, allowed = block_view(block_start)
        query_block = queries
        scores = jnp.einsum(
            "qhd,khd->hqk", query_block, key_all, preferred_element_type=jnp.float32
        )
        scores = jnp.where(allowed[None], scores, masked_score)
        row_max = jnp.max(scores, axis=-1, keepdims=True)
        exponent = jnp.exp(scores - row_max)
        row_total = jnp.sum(exponent, axis=-1, keepdims=True)
        probability = (exponent / row_total).astype(jnp.bfloat16)
        log_totals.append(row_max + jnp.log(row_total))
        attended_parts.append(
            jnp.einsum("hqk,khd->qhd", probability, value_all, preferred_element_type=jnp.float32)
        )
    attended = attended_parts[0].reshape(tok_count, D).astype(jnp.bfloat16)
    residual = tokens_wide + jnp.dot(attended, collector_all, preferred_element_type=jnp.float32)
    second_scale = norm_scale(residual)
    hidden_in = (residual * second_scale * second_wide).astype(jnp.bfloat16)
    hidden_wide = hidden_in.astype(jnp.float32)
    logits = jnp.dot(hidden_in, router_all, preferred_element_type=jnp.float32) + jnp.dot(
        past_logits, carryover, precision=highest, preferred_element_type=jnp.float32
    )
    gate_values = softmax_rows(jnp.take_along_axis(logits, routes, axis=1))
    onehot = (
        routes[:, :, None] == jnp.arange(expert_count, dtype=jnp.int32)[None, None, :]
    ).astype(jnp.int32)
    per_token = jnp.sum(onehot, axis=1)
    before = jnp.cumsum(per_token, axis=0) - per_token
    position_in = jnp.sum(onehot * before[:, None, :], axis=2)
    dump_slot = expert_count * CAP
    slot_index = jnp.where(routes < expert_count, routes * CAP + position_in, dump_slot)
    slot_table = (
        jnp.full((dump_slot + 1,), 2 * tok_count, jnp.int32)
        .at[slot_index.reshape(-1)]
        .set(jnp.arange(2 * tok_count, dtype=jnp.int32))[:dump_slot]
    )
    zero_row = jnp.zeros((1, D), jnp.bfloat16)
    send_rows = jnp.concatenate([hidden_in, zero_row], axis=0)[slot_table // 2].reshape(
        expert_count, CAP, D
    )
    received_rows = lax.all_to_all(send_rows, "expert", split_axis=0, concat_axis=0, tiled=True)
    answered = expert_forward(received_rows, gating_all, upward_all, downward_all)
    answer_back = lax.all_to_all(answered, "expert", split_axis=0, concat_axis=0, tiled=True)
    expert_values = jnp.concatenate([answer_back.reshape(-1, D), zero_row], axis=0)[
        slot_index
    ].astype(jnp.float32)
    mixing = softmax_rows(
        jnp.dot(hidden_in, blender_all, preferred_element_type=jnp.float32).reshape(tok_count, 2, 2)
    )
    const_values = (
        mixing[:, :, 0:1] * hidden_wide[:, None, :]
        + mixing[:, :, 1:2] * constants_wide.T[None, :, :]
    )
    route_copy = (routes == expert_count + 1).astype(jnp.float32)[:, :, None]
    route_first = (routes == expert_count + 2).astype(jnp.float32)[:, :, None]
    route_second = (routes == expert_count + 3).astype(jnp.float32)[:, :, None]
    values_all = (
        expert_values
        + route_copy * hidden_wide[:, None, :]
        + route_first * const_values[:, 0:1, :]
        + route_second * const_values[:, 1:2, :]
    )
    layer_output = (residual + jnp.sum(gate_values[:, :, None] * values_all, axis=1)).astype(
        jnp.bfloat16
    )
    upstream = cotangent.astype(jnp.float32)
    value_grad = gate_values[:, :, None] * upstream[:, None, :]
    gate_grad = jnp.sum(values_all * upstream[:, None, :], axis=2)
    chosen_grad = gate_values * (
        gate_grad - jnp.sum(gate_values * gate_grad, axis=1, keepdims=True)
    )
    all_experts = jnp.arange(expert_count + 4, dtype=jnp.int32)
    logit_grad = jnp.sum(
        (routes[:, :, None] == all_experts[None, None, :]).astype(jnp.float32)
        * chosen_grad[:, :, None],
        axis=1,
    )
    grad_rows = jnp.concatenate(
        [value_grad.reshape(2 * tok_count, D).astype(jnp.bfloat16), zero_row], axis=0
    )[slot_table].reshape(expert_count, CAP, D)
    refetched = (
        lax.all_gather(gating, "fsdp", axis=1, tiled=True),
        lax.all_gather(upward, "fsdp", axis=1, tiled=True),
        lax.all_gather(downward, "fsdp", axis=1, tiled=True),
    )
    gating_use, upward_use, downward_use = (refetched[0][0], refetched[1][0], refetched[2][0])
    rows_back, grads_back = (
        lax.all_to_all(send_rows, "expert", split_axis=0, concat_axis=0, tiled=True),
        lax.all_to_all(grad_rows, "expert", split_axis=0, concat_axis=0, tiled=True),
    )
    flat_rows = rows_back.reshape(-1, D)
    flat_grads = grads_back.reshape(-1, D)
    gate_pre = jnp.dot(flat_rows, gating_use, preferred_element_type=jnp.float32)
    up_pre = jnp.dot(flat_rows, upward_use, preferred_element_type=jnp.float32)
    sigmoid_gate = jax.nn.sigmoid(gate_pre)
    activated = jax.nn.silu(gate_pre)
    hidden = (activated * up_pre).astype(jnp.bfloat16)
    hidden_grad = jnp.dot(flat_grads, downward_use, preferred_element_type=jnp.float32)
    gate_low = (
        hidden_grad * up_pre * sigmoid_gate * (1.0 + gate_pre * (1.0 - sigmoid_gate))
    ).astype(jnp.bfloat16)
    up_low = (hidden_grad * activated).astype(jnp.bfloat16)
    rows_grad = lax.dot_general(
        gate_low, gating_use, contract_cols, preferred_element_type=jnp.float32
    ) + lax.dot_general(up_low, upward_use, contract_cols, preferred_element_type=jnp.float32)
    returned_grads = lax.all_to_all(
        rows_grad.astype(jnp.bfloat16).reshape(expert_count, CAP, D),
        "expert",
        split_axis=0,
        concat_axis=0,
        tiled=True,
    )
    both_low = jnp.concatenate([gate_low, up_low], axis=1)
    inward = lax.dot_general(flat_rows, both_low, contract_rows, preferred_element_type=jnp.float32)
    outward = lax.dot_general(flat_grads, hidden, contract_rows, preferred_element_type=jnp.float32)
    expert_sums = lax.psum_scatter(
        jnp.concatenate([inward, outward], axis=1).astype(jnp.bfloat16),
        "fsdp",
        scatter_dimension=0,
        tiled=True,
    ).astype(jnp.float32)
    gradient_gating = expert_sums[:, :FF][None]
    gradient_upward = expert_sums[:, FF : 2 * FF][None]
    gradient_downward = expert_sums[:, 2 * FF :][None]
    returned_rows = jnp.concatenate([returned_grads.reshape(-1, D), zero_row], axis=0)[
        slot_index
    ].astype(jnp.float32)
    const_grad = jnp.stack(
        [jnp.sum(route_first * value_grad, axis=1), jnp.sum(route_second * value_grad, axis=1)],
        axis=1,
    )
    mixing_grad = jnp.stack(
        [
            jnp.sum(const_grad * hidden_wide[:, None, :], axis=2),
            jnp.sum(const_grad * constants_wide.T[None, :, :], axis=2),
        ],
        axis=2,
    )
    blend_grad = (
        mixing * (mixing_grad - jnp.sum(mixing * mixing_grad, axis=2, keepdims=True))
    ).reshape(tok_count, 4)
    constants_grad = jnp.sum(const_grad * mixing[:, :, 1:2], axis=0).T
    hidden_grad_sum = (
        jnp.sum(returned_rows, axis=1)
        + jnp.sum(route_copy * value_grad, axis=1)
        + jnp.sum(const_grad * mixing[:, :, 0:1], axis=1)
    )
    hidden_grad_sum = hidden_grad_sum + lax.dot_general(
        blend_grad,
        blender_wide,
        contract_cols,
        precision=highest,
        preferred_element_type=jnp.float32,
    )
    hidden_grad_sum = hidden_grad_sum + lax.dot_general(
        logit_grad,
        router_wide,
        contract_cols,
        precision=highest,
        preferred_element_type=jnp.float32,
    )
    blender_grad = lax.dot_general(
        hidden_wide,
        blend_grad,
        contract_rows,
        precision=highest,
        preferred_element_type=jnp.float32,
    )
    router_grad = lax.dot_general(
        hidden_wide,
        logit_grad,
        contract_rows,
        precision=highest,
        preferred_element_type=jnp.float32,
    )
    carryover_local = lax.dot_general(
        past_logits,
        logit_grad,
        contract_rows,
        precision=highest,
        preferred_element_type=jnp.float32,
    )
    gradient_logits = lax.dot_general(
        logit_grad, carryover, contract_cols, precision=highest, preferred_element_type=jnp.float32
    )
    second_grad = jnp.sum(hidden_grad_sum * residual * second_scale, axis=0)
    scaled_two = hidden_grad_sum * second_wide
    residual_grad = (
        upstream
        + second_scale * scaled_two
        - residual
        * (second_scale * second_scale * second_scale)
        * jnp.mean(scaled_two * residual, axis=-1, keepdims=True)
    )
    residual_low = residual_grad.astype(jnp.bfloat16)
    collector_grad = lax.dot_general(
        attended, residual_low, contract_rows, preferred_element_type=jnp.float32
    )
    attended_grad = (
        lax.dot_general(
            residual_low, collector_all, contract_cols, preferred_element_type=jnp.float32
        )
        .astype(jnp.bfloat16)
        .reshape(tok_count, H, HD)
    )
    key_grad_all = jnp.zeros((span_rows, H, HD), jnp.float32)
    value_grad_all = jnp.zeros((span_rows, H, HD), jnp.float32)
    query_parts = []
    for block_number, block_start in enumerate(block_starts):
        key_start, allowed = block_view(block_start)
        query_block = queries
        scores = jnp.einsum(
            "qhd,khd->hqk", query_block, key_all, preferred_element_type=jnp.float32
        )
        scores = jnp.where(allowed[None], scores, masked_score)
        probability = jnp.exp(scores - log_totals[block_number])
        prob_grad = jnp.einsum(
            "qhd,khd->hqk", attended_grad, value_all, preferred_element_type=jnp.float32
        )
        row_delta = jnp.sum(prob_grad * probability, axis=-1, keepdims=True)
        score_grad = (probability * (prob_grad - row_delta)).astype(jnp.bfloat16)
        query_parts.append(
            jnp.einsum("hqk,khd->qhd", score_grad, key_all, preferred_element_type=jnp.float32)
        )
        key_grad_all = key_grad_all.at[key_start : key_start + key_span].add(
            jnp.einsum("hqk,qhd->khd", score_grad, query_block, preferred_element_type=jnp.float32)
        )
        value_grad_all = value_grad_all.at[key_start : key_start + key_span].add(
            jnp.einsum(
                "hqk,qhd->khd",
                probability.astype(jnp.bfloat16),
                attended_grad,
                preferred_element_type=jnp.float32,
            )
        )
    key_grad_own = key_grad_all[HOPS * tok_count :].reshape(tok_count, D)
    value_grad_own = value_grad_all[HOPS * tok_count :].reshape(tok_count, D)
    for hop_count in range(1, HOPS + 1):
        segment = (HOPS - hop_count) * tok_count
        key_back, value_back = (
            shifted(
                key_grad_all[segment : segment + tok_count]
                .reshape(tok_count, D)
                .astype(jnp.bfloat16),
                "fsdp",
                -hop_count,
            ).astype(jnp.float32),
            shifted(
                value_grad_all[segment : segment + tok_count]
                .reshape(tok_count, D)
                .astype(jnp.bfloat16),
                "fsdp",
                -hop_count,
            ).astype(jnp.float32),
        )
        key_grad_own = key_grad_own + key_back
        value_grad_own = value_grad_own + value_back
    query_grad = rotate_back(query_parts[0], cosine_table, sine_table) * query_scale
    key_grad = rotate_back(key_grad_own.reshape(tok_count, H, HD), cosine_table, sine_table)
    projected_grad = (
        jnp.stack([query_grad, key_grad, value_grad_own.reshape(tok_count, H, HD)], axis=1)
        .reshape(tok_count, 3 * D)
        .astype(jnp.bfloat16)
    )
    projector_grad = lax.dot_general(
        normed, projected_grad, contract_rows, preferred_element_type=jnp.float32
    )
    normed_grad = lax.dot_general(
        projected_grad, projector_all, contract_cols, preferred_element_type=jnp.float32
    )
    first_grad = jnp.sum(normed_grad * tokens_wide * first_scale, axis=0)
    scaled_one = normed_grad * first_wide
    gradient_tokens = (
        residual_grad
        + first_scale * scaled_one
        - tokens_wide
        * (first_scale * first_scale * first_scale)
        * jnp.mean(scaled_one * tokens_wide, axis=-1, keepdims=True)
    ).astype(jnp.bfloat16)
    shared_sums = (
        lax.psum_scatter(
            projector_grad.astype(jnp.bfloat16), "fsdp", scatter_dimension=0, tiled=True
        ).astype(jnp.float32),
        lax.psum_scatter(
            collector_grad.astype(jnp.bfloat16), "fsdp", scatter_dimension=0, tiled=True
        ).astype(jnp.float32),
        lax.psum_scatter(
            router_grad.astype(jnp.bfloat16), "fsdp", scatter_dimension=0, tiled=True
        ).astype(jnp.float32),
        lax.psum_scatter(
            blender_grad.astype(jnp.bfloat16), "fsdp", scatter_dimension=0, tiled=True
        ).astype(jnp.float32),
        lax.psum_scatter(
            constants_grad.astype(jnp.bfloat16), "fsdp", scatter_dimension=0, tiled=True
        ).astype(jnp.float32),
        lax.psum_scatter(
            first_grad.astype(jnp.bfloat16), "fsdp", scatter_dimension=0, tiled=True
        ).astype(jnp.float32),
        lax.psum_scatter(
            second_grad.astype(jnp.bfloat16), "fsdp", scatter_dimension=0, tiled=True
        ).astype(jnp.float32),
    )
    shared_sums = (
        lax.psum(shared_sums[0].astype(jnp.bfloat16), "expert").astype(jnp.float32),
        lax.psum(shared_sums[1].astype(jnp.bfloat16), "expert").astype(jnp.float32),
        lax.psum(shared_sums[2].astype(jnp.bfloat16), "expert").astype(jnp.float32),
        lax.psum(shared_sums[3].astype(jnp.bfloat16), "expert").astype(jnp.float32),
        lax.psum(shared_sums[4].astype(jnp.bfloat16), "expert").astype(jnp.float32),
        lax.psum(shared_sums[5].astype(jnp.bfloat16), "expert").astype(jnp.float32),
        lax.psum(shared_sums[6].astype(jnp.bfloat16), "expert").astype(jnp.float32),
    )
    gradient_carryover = lax.psum(carryover_local, ("expert", "fsdp"))
    return (
        layer_output,
        gradient_tokens,
        gradient_logits,
        shared_sums[0],
        shared_sums[1],
        shared_sums[2],
        shared_sums[3],
        shared_sums[4],
        shared_sums[5],
        shared_sums[6],
        gradient_carryover,
        gradient_gating,
        gradient_upward,
        gradient_downward,
    )


def solution(mesh):
    return jax.shard_map(
        local,
        mesh=mesh,
        in_specs=(
            P(("expert", "fsdp"), None),
            P(("expert", "fsdp"), None),
            P(("expert", "fsdp"), None),
            P("expert", None),
            P("fsdp", None),
            P("fsdp", None),
            P("fsdp", None),
            P("fsdp", None),
            P("fsdp", None),
            P("fsdp"),
            P("fsdp"),
            P(),
            P("expert", "fsdp", None),
            P("expert", "fsdp", None),
            P("expert", "fsdp", None),
            P(("expert", "fsdp"), None),
        ),
        out_specs=(
            P(("expert", "fsdp"), None),
            P(("expert", "fsdp"), None),
            P(("expert", "fsdp"), None),
            P("fsdp", None),
            P("fsdp", None),
            P("fsdp", None),
            P("fsdp", None),
            P("fsdp", None),
            P("fsdp"),
            P("fsdp"),
            P(),
            P("expert", "fsdp", None),
            P("expert", "fsdp", None),
            P("expert", "fsdp", None),
        ),
        check_vma=False,
    )
```

profile of v0, /device:TPU:0, one launch (start us, length us, event | category | flops | bytes accessed | tf_op | source)
XLA Modules:
  0.0 817.7 jit_solution(515937530792381711)
XLA Ops:
  14.9 18.7 %all-reduce.9 = (bf16[768]{0:T(1024)(128)(2,1)S(1)}, bf16[768]{0:T(1024)(128)(2,1)S(1)}) all-reduce(bf16[768]{0:T(1024)(128)(2,1)S(1)} %dynamic-update-slice.4, bf16[768]{0:T(1024)(128)(2,1)S(1)} %dynamic-update-slice.5), channel_id=1, replica_groups=mesh['expert'=4,'fsdp'=8] {'fsdp'}, use_global_device_ids=true, to_apply=%add.4 | all-reduce | flops 1536 | bytes 6144
  34.1 8.4 %all-gather.2 = bf16[8,96,2]{1,2,0:T(2,128)(2,1)S(1)} all-gather(bf16[1,96,2]{1,2,0:T(2,128)(2,1)S(1)} %bitcast.213), channel_id=1, replica_groups=mesh['expert'=4,'fsdp'=8] {'fsdp'}, dimensions={0}, use_global_device_ids=true | all-gather | bytes 3456 | tf_op jit(solution)/shard_map/all_gather | solution.py:123
  45.4 11.1 %all-gather.1 = bf16[8,96,4]{1,2,0:T(4,128)(2,1)S(1)} all-gather(bf16[1,96,4]{1,2,0:T(4,128)(2,1)S(1)} %bitcast.212), channel_id=1, replica_groups=mesh['expert'=4,'fsdp'=8] {'fsdp'}, dimensions={0}, use_global_device_ids=true | all-gather | bytes 6912 | tf_op jit(solution)/shard_map/all_gather | solution.py:122
  56.6 12.7 %all-gather = bf16[8,96,8]{1,2,0:T(8,128)(2,1)S(1)} all-gather(bf16[1,96,8]{1,2,0:T(8,128)(2,1)S(1)} %bitcast.209), channel_id=1, replica_groups=mesh['expert'=4,'fsdp'=8] {'fsdp'}, dimensions={0}, use_global_device_ids=true | all-gather | bytes 13824 | tf_op jit(solution)/shard_map/all_gather | solution.py:121
  104.7 25.0 %collective-permute-done.2 = bf16[512,768]{0,1:T(8,128)(2,1)S(1)} collective-permute-done((bf16[512,768]{0,1:T(8,128)(2,1)S(1)}, bf16[512,768]{0,1:T(8,128)(2,1)S(1)}, u32[]{:S(2)}, u32[]{:S(2)}) %collective-permute-start.2) | collective-permute-done | bytes 786464 | tf_op jit(solution)/shard_map/ppermute | solution.py:27
  130.6 17.0 %select_reduce_fusion = (f32[12,512]{1,0:T(8,128)S(1)}, f32[12,512,1536]{2,1,0:T(8,128)}) fusion(pred[512,1536]{1,0:T(8,128)(4,1)S(1)} %fusion.32, bf16[512,12,64]{0,2,1:T(8,128)(2,1)S(1)} %maximum_convert_fusion, bf16[512,12,64]{0,2,1:T(8,128)(2,1)} %bitcast.184, bf16[512,12,64]{0,2,1:T(8,128)(2,1)} %bitcast.186, ...), kind=kOutput, calls=%fused_computation.12 | convolution fusion | flops 1235085312 | bytes 42491904 | tf_op jit(solution)/shard_map/qhd,khd->hqk/dot_general | solution.py:186
  147.6 17.2 %fusion = f32[12,512]{1,0:T(8,128)S(1)} fusion(f32[12,512,1536]{2,1,0:T(8,128)} %get-tuple-element.224, f32[12,512]{1,0:T(8,128)S(1)} %get-tuple-element.223, pred[512,1536]{1,0:T(8,128)(4,1)S(1)} %fusion.32), kind=kLoop, calls=%fused_computation.11 | loop fusion | flops 28305408 | bytes 38584320 | tf_op jit(solution)/shard_map/reduce_sum | solution.py:192
  164.9 16.4 %fusion.52 = bf16[12,64,512]{2,1,0:T(8,128)(2,1)S(1)} fusion(f32[12,512,1536]{2,1,0:T(8,128)} %get-tuple-element.224, f32[12,512]{1,0:T(8,128)S(1)} %fusion, f32[12,512]{1,0:T(8,128)S(1)} %get-tuple-element.223, pred[512,1536]{1,0:T(8,128)(4,1)S(1)} %fusion.32, bf16[512,12,64]{0,2,1:T(8,128)(2,1)S(1)} %copy-done.19, bf16[512,12,64]{0,2,1:T(8,128)(2,1)} %bitcast.4, ...), kind=kOutput, calls=%fused_computation.111 | convolution fusion | flops 1253179392 | bytes 41730048 | tf_op jit(solution)/shard_map/hqk,khd->qhd/dot_general | solution.py:196
  187.8 6.5 gather_fusion.4
  224.0 5.9 fusion.18
  230.0 9.5 %multiply_convert_fusion.2 = (bf16[512,2048]{1,0:T(8,128)(2,1)S(1)}, bf16[512,2048]{1,0:T(8,128)(2,1)S(1)}, bf16[512,2048]{1,0:T(8,128)(2,1)}) fusion(f32[512,2048]{1,0:T(8,128)} %fusion.18, f32[512,2048]{1,0:T(8,128)} %fusion.24, bf16[512,768]{1,0:T(8,128)(2,1)} %bitcast.21, bf16[1,768,2048]{2,1,0:T(8,128)(2,1)} %all-gather.13.cloned.1.call-done), kind=kOutput, calls=%fused_computation.31 | convolution fusion | flops 1626341376 | bytes 18612224 | tf_op jit(solution)/shard_map/dot_general | solution.py:87
  250.0 6.7 fusion.85
  297.3 25.2 %multiply_reduce_fusion.2 = (f32[512,2]{1,0:T(8,128)}, f32[512,768]{1,0:T(8,128)}, f32[512,768]{1,0:T(8,128)}, f32[512,768]{1,0:T(8,128)}, f32[512,768]{1,0:T(8,128)}) fusion(f32[512,768]{1,0:T(8,128)} %convert_element_type.257, f32[512,2]{1,0:T(8,128)S(1)} %copy.169, f32[512,2]{1,0:T(8,128)S(1)} %copy-done.35, f32[512,2]{1,0:T(8,128)S(1)} %copy-done.34, ...), kind=kLoop, calls=%fused_computation.61 | loop fusion | flops 11795456 | bytes 15749120 | tf_op jit(solution)/shard_map/reduce_sum | solution.py:251
  327.5 12.8 %multiply_reduce_fusion.1 = (bf16[2,768]{1,0:T(2,128)(2,1)S(1)}, f32[512,2]{1,0:T(8,128)S(1)}, f32[512,2]{1,0:T(8,128)S(1)}, f32[512,768]{1,0:T(8,128)}) fusion(f32[512,2]{1,0:T(8,128)S(1)} %bitcast.193, f32[512,1,768]{2,1,0:T(1,128)S(1)} %stack.28, f32[512,1,768]{2,1,0:T(1,128)S(1)} %stack.27, f32[512,768]{1,0:T(8,128)S(1)} %copy-done.6, ...), kind=kLoop, calls=%fused_computation.60 | loop fusion | flops 6681088 | bytes 6317056 | tf_op jit(solution)/shard_map/reduce_sum | solution.py:325
  342.7 6.9 reduce_sum.253
  362.0 18.7 %fusion.90 = (bf16[1536,12,64]{0,2,1:T(8,128)(2,1)}, f32[1536,12,64]{0,2,1:T(8,128)}) fusion(bf16[512,12,64]{0,2,1:T(8,128)(2,1)S(1)} %bitcast.176, f32[12,512,1536]{2,1,0:T(8,128)} %get-tuple-element.224, f32[12,512]{1,0:T(8,128)S(1)} %log_add_fusion, pred[512,1536]{1,0:T(8,128)(4,1)S(1)} %fusion.32), kind=kOutput, calls=%fused_computation.213 | convolution fusion | flops 1237450752 | bytes 46424064 | tf_op jit(solution)/shard_map/hqk,qhd->khd/dot_general | solution.py:412
  380.7 27.0 %multiply_reduce_fusion = (f32[12,512]{1,0:T(8,128)S(1)}, f32[12,512,1536]{2,1,0:T(8,128)}) fusion(f32[12,512,1536]{2,1,0:T(8,128)} %get-tuple-element.224, f32[12,512]{1,0:T(8,128)S(1)} %log_add_fusion, pred[512,1536]{1,0:T(8,128)(4,1)S(1)} %fusion.32, bf16[512,12,64]{0,2,1:T(8,128)(2,1)S(1)} %bitcast.177, bf16[512,12,64]{0,2,1:T(8,128)(2,1)S(1)} %copy-done.20, ...), kind=kOutput, calls=%fused_computation.7 | convolution fusion | flops 1252780032 | bytes 79478784 | tf_op jit(solution)/shard_map/qhd,khd->hqk/dot_general | solution.py:400
  407.8 24.2 %multiply_convert_fusion = bf16[12,512,1536]{2,1,0:T(8,128)(2,1)S(1)} fusion(f32[12,512,1536]{2,1,0:T(8,128)} %get-tuple-element.231, f32[12,512,1536]{2,1,0:T(8,128)} %get-tuple-element.224, f32[12,512]{1,0:T(8,128)S(1)} %get-tuple-element.230, f32[12,512]{1,0:T(8,128)S(1)} %log_add_fusion, pred[512,1536]{1,0:T(8,128)(4,1)S(1)} %fusion.32), kind=kLoop, calls=%fused_computation.6 | loop fusion | flops 47185920 | bytes 95207424 | tf_op jit(solution)/shard_map/convert_element_type | solution.py:404
  432.1 7.9 fusion.91
  446.3 10.1 %convolution_bitcast_fusion.1 = f32[512,12,64]{0,2,1:T(8,128)S(1)} fusion(bf16[12,512,1536]{2,1,0:T(8,128)(2,1)} %copy-done.1, bf16[512,12,64]{0,2,1:T(8,128)(2,1)S(1)} %copy-done.11, bf16[512,12,64]{0,2,1:T(8,128)(2,1)} %bitcast.185, bf16[512,12,64]{0,2,1:T(8,128)(2,1)} %bitcast.187), kind=kOutput, calls=%fused_computation.108 | convolution fusion | flops 1215037440 | bytes 22806528 | tf_op jit(solution)/shard_map/hqk,khd->qhd/dot_general | solution.py:406
  462.4 8.2 collective-permute-done.5
  473.1 29.9 %collective-permute-done.7 = bf16[512,768]{0,1:T(8,128)(2,1)S(1)} collective-permute-done((bf16[512,768]{0,1:T(8,128)(2,1)S(1)}, bf16[512,768]{0,1:T(8,128)(2,1)S(1)}, u32[]{:S(2)}, u32[]{:S(2)}) %collective-permute-start.7) | collective-permute-done | bytes 786464 | tf_op jit(solution)/shard_map/ppermute | solution.py:27
  510.8 7.9 convolution_convert_fusion
  526.0 37.9 %reduce-scatter.13.cloned.1.call-done = bf16[96,2304]{1,0:T(8,128)(2,1)} async-done(((bf16[768,2304]{1,0:T(8,128)(2,1)}), bf16[96,2304]{1,0:T(8,128)(2,1)}) %reduce-scatter.13.cloned.1.call-update) | async-done | bytes 442384 | tf_op jit(solution)/shard_map/reduce_scatter | solution.py:464
  563.9 7.0 pad_maximum_fusion
  571.9 37.9 %psum.63 = f32[8,8]{0,1:T(8,128)S(1)} all-reduce(f32[8,8]{0,1:T(8,128)S(1)} %convolution_bitcast_fusion.2), channel_id=1, replica_groups=mesh['expert'=4,'fsdp'=8] {'expert','fsdp'}, use_global_device_ids=true, to_apply=%region_48.49 | all-reduce | flops 64 | bytes 512 | tf_op jit(solution)/shard_map/psum | solution.py:495
  612.0 14.9 %reduce-scatter.21.cloned.1.call-done = bf16[96,4]{1,0:T(8,128)(2,1)} async-done(((bf16[768,4]{1,0:T(8,128)(2,1)}), bf16[96,4]{1,0:T(8,128)(2,1)}) %reduce-scatter.21.cloned.1.call-update) | async-done | bytes 784
  627.7 30.4 %reduce-scatter.19.cloned.1.call-done = bf16[96,8]{1,0:T(8,128)(2,1)} async-done(((bf16[768,8]{1,0:T(8,128)(2,1)}), bf16[96,8]{1,0:T(8,128)(2,1)}) %reduce-scatter.19.cloned.1.call-update) | async-done | bytes 1552
  664.4 13.8 %all-reduce.8 = (bf16[768]{0:T(1024)(128)(2,1)S(1)}, bf16[768]{0:T(1024)(128)(2,1)S(1)}) all-reduce(bf16[768]{0:T(1024)(128)(2,1)S(1)} %get-tuple-element.160, bf16[768]{0:T(1024)(128)(2,1)S(1)} %get-tuple-element.152), channel_id=7, replica_groups=mesh['expert'=4,'fsdp'=8] {'fsdp'}, use_global_device_ids=true, to_apply=%region_43.44.clone | all-reduce | flops 1536 | bytes 6144
  678.3 10.2 %all-reduce.10 = (bf16[96,8]{0,1:T(8,128)(2,1)S(1)}, bf16[96,4]{0,1:T(4,128)(2,1)S(1)}, bf16[96,2]{0,1:T(2,128)(2,1)S(1)}, bf16[96]{0:T(256)(128)(2,1)S(1)}, bf16[96]{0:T(256)(128)(2,1)S(1)}) all-reduce(bf16[96,8]{0,1:T(8,128)(2,1)S(1)} %copy.190, bf16[96,4]{0,1:T(4,128)(2,1)S(1)} %copy.192, ...), channel_id=1, replica_groups=mesh['expert'=4,'fsdp'=8] {'expert'}, use_global_device_ids=true, to_apply=%region_36.37 | all-reduce | flops 1536 | bytes 6144 | tf_op jit(solution)/shard_map/psum | solution.py:489
  694.5 11.4 %all-reduce.14.cloned.1.call-done = (bf16[96,2304]{1,0:T(8,128)(2,1)}, bf16[96,768]{1,0:T(8,128)(2,1)}) async-done(((bf16[96,2304]{1,0:T(8,128)(2,1)}, bf16[96,768]{1,0:T(8,128)(2,1)}), (bf16[96,2304]{1,0:T(8,128)(2,1)}, bf16[96,768]{1,0:T(8,128)(2,1)})) %all-reduce.14.cloned.1.call-update) | async-done | bytes 589840 | tf_op jit(solution)/shard_map/psum | solution.py:487
  709.6 98.2 %reduce-scatter.17.cloned.1.call-done = bf16[96,6144]{1,0:T(8,128)(2,1)} async-done(((bf16[768,6144]{1,0:T(8,128)(2,1)}), bf16[96,6144]{1,0:T(8,128)(2,1)}) %reduce-scatter.17.cloned.1.call-update) | async-done | bytes 1179664 | tf_op jit(solution)/shard_map/reduce_scatter | solution.py:299
  (377 shorter events, 204.6 us)
Async XLA Ops:
  7.2 180.4 %copy-start = (f32[512,8]{0,1:T(8,128)S(1)}, f32[512,8]{0,1:T(8,128)}, u32[]{:S(2)}) copy-start(f32[512,8]{0,1:T(8,128)} %param.25) | copy-start | bytes 49156
  7.3 78.8 %all-gather.9.cloned.1.call-start = ((), (), s32[]{:S(2)}) async-start(), calls=%async_computation.10 | async-start | bytes 3981312 | tf_op jit(solution)/shard_map/all_gather | solution.py:119
  8.0 173.3 %all-gather.11.cloned.1.call-start = ((), (), s32[]{:S(2)}) async-start(), calls=%async_computation.11 | async-start | bytes 1327104 | tf_op jit(solution)/shard_map/all_gather | solution.py:120
  8.8 68.6 %copy-start.15 = (bf16[512,768]{1,0:T(8,128)(2,1)S(1)}, bf16[512,768]{1,0:T(8,128)(2,1)}, u32[]{:S(2)}) copy-start(bf16[512,768]{1,0:T(8,128)(2,1)} %param.39) | copy-start | bytes 2359300
  8.8 209.3 %all-gather.15.cloned.1.call-start = ((), (), s32[]{:S(2)}) async-start(), calls=%async_computation.13 | async-start | bytes 3538944 | tf_op jit(solution)/shard_map/all_gather | solution.py:137
  9.5 214.5 %all-gather.17.cloned.1.call-start = ((), (), s32[]{:S(2)}) async-start(), calls=%async_computation.14 | async-start | bytes 3538944 | tf_op jit(solution)/shard_map/all_gather | solution.py:138
  10.1 219.9 %all-gather.13.cloned.1.call-start = ((), (), s32[]{:S(2)}) async-start(), calls=%async_computation.12 | async-start | bytes 3538944 | tf_op jit(solution)/shard_map/all_gather | solution.py:136
  33.5 52.6 %copy-start.61 = (f32[768]{0:T(1024)}, f32[768]{0:T(1024)S(1)}, u32[]{:S(2)}) copy-start(f32[768]{0:T(1024)S(1)} %convert_element_type.230) | copy-start | bytes 9220
  34.1 52.0 %copy-start.66 = (f32[512]{0:T(512)}, f32[512]{0:T(512)S(1)}, u32[]{:S(2)}) copy-start(f32[512]{0:T(512)S(1)} %get-tuple-element.218) | copy-start | bytes 6148
  56.6 129.8 %copy-start.49 = (bf16[768,4]{0,1:T(4,128)(2,1)}, bf16[768,4]{0,1:T(4,128)(2,1)S(1)}, u32[]{:S(2)}) copy-start(bf16[768,4]{0,1:T(4,128)(2,1)S(1)} %reshape.619) | copy-start | bytes 18436
  91.5 13.3 %collective-permute-start.3 = (bf16[512,768]{0,1:T(8,128)(2,1)S(1)}, bf16[512,768]{0,1:T(8,128)(2,1)S(1)}, u32[]{:S(2)}, u32[]{:S(2)}) collective-permute-start(bf16[512,768]{0,1:T(8,128)(2,1)S(1)} %bitcast.178), channel_id=1, source_target_pairs={{0,1},{1,2},{2,3},{3,4},{4,5},{5,6},{6,7},{8,9},{9,10},{10,11},{11... | collective-permute-start | bytes 2359304 | tf_op jit(solution)/shard_map/ppermute | solution.py:27
  93.7 36.0 %collective-permute-start.2 = (bf16[512,768]{0,1:T(8,128)(2,1)S(1)}, bf16[512,768]{0,1:T(8,128)(2,1)S(1)}, u32[]{:S(2)}, u32[]{:S(2)}) collective-permute-start(bf16[512,768]{0,1:T(8,128)(2,1)S(1)} %bitcast.179), channel_id=1, source_target_pairs={{0,2},{1,3},{2,4},{3,5},{4,6},{5,7},{8,10},{9,11},{10,12},{11,13},... | collective-permute-start | bytes 2359304 | tf_op jit(solution)/shard_map/ppermute | solution.py:27
  96.7 68.2 %collective-permute-start.1 = (bf16[512,768]{0,1:T(8,128)(2,1)}, bf16[512,768]{0,1:T(8,128)(2,1)}, u32[]{:S(2)}, u32[]{:S(2)}) collective-permute-start(bf16[512,768]{0,1:T(8,128)(2,1)} %bitcast.2), channel_id=1, source_target_pairs={{0,1},{1,2},{2,3},{3,4},{4,5},{5,6},{6,7},{8,9},{9,10},{10,11},{11... | collective-permute-start | bytes 2359304 | tf_op jit(solution)/shard_map/ppermute | solution.py:27
  100.9 63.9 %collective-permute-start = (bf16[512,768]{0,1:T(8,128)(2,1)}, bf16[512,768]{0,1:T(8,128)(2,1)}, u32[]{:S(2)}, u32[]{:S(2)}) collective-permute-start(bf16[512,768]{0,1:T(8,128)(2,1)} %bitcast.2), channel_id=1, source_target_pairs={{0,2},{1,3},{2,4},{3,5},{4,6},{5,7},{8,10},{9,11},{10,12},{11,13},... | collective-permute-start | bytes 2359304 | tf_op jit(solution)/shard_map/ppermute | solution.py:27
  197.4 12.7 %all-to-all-start = ((bf16[4,128,768]{2,1,0:T(8,128)(2,1)}), bf16[4,128,768]{2,1,0:T(8,128)(2,1)}, u32[]{:S(2)}, u32[]{:S(2)}) async-start(bf16[4,128,768]{2,1,0:T(8,128)(2,1)} %bitcast.20), calls=%async_computation | async-start | bytes 1572864 | tf_op jit(solution)/shard_map/all_to_all | solution.py:224
  202.2 54.4 %copy-start.47 = (f32[512,2]{0,1:T(2,128)}, f32[512,2]{0,1:T(2,128)S(1)}, u32[]{:S(2)}) copy-start(f32[512,2]{0,1:T(2,128)S(1)} %fusion.64) | copy-start | bytes 12292
  210.1 13.9 %all-to-all-start.2 = ((bf16[4,128,768]{2,1,0:T(8,128)(2,1)}), bf16[4,128,768]{2,1,0:T(8,128)(2,1)}, u32[]{:S(2)}, u32[]{:S(2)}) async-start(bf16[4,128,768]{2,1,0:T(8,128)(2,1)} %bitcast.32), calls=%async_computation.2 | async-start | bytes 1572864 | tf_op jit(solution)/shard_map/all_to_all | solution.py:272
  245.6 17.5 %all-to-all-start.3 = ((bf16[4,128,768]{2,1,0:T(8,128)(2,1)}), bf16[4,128,768]{2,1,0:T(8,128)(2,1)S(1)}, u32[]{:S(2)}, u32[]{:S(2)}) async-start(bf16[4,128,768]{2,1,0:T(8,128)(2,1)} %bitcast.34), calls=%async_computation.3 | async-start | bytes 1572864 | tf_op jit(solution)/shard_map/all_to_all | solution.py:289
  263.1 12.6 %all-to-all-start.1 = ((bf16[4,128,768]{2,1,0:T(8,128)(2,1)}), bf16[4,128,768]{2,1,0:T(8,128)(2,1)}, u32[]{:S(2)}, u32[]{:S(2)}) async-start(bf16[4,128,768]{2,1,0:T(8,128)(2,1)} %bitcast.200), calls=%async_computation.1 | async-start | bytes 1572864 | tf_op jit(solution)/shard_map/all_to_all | solution.py:226
  267.4 258.6 %reduce-scatter.15.cloned.1.call-start = ((), (), s32[]{:S(2)}) async-start(), calls=%async_computation.16 | async-start | bytes 1327104 | tf_op jit(solution)/shard_map/reduce_scatter | solution.py:467
  407.8 156.1 %reduce-scatter.13.cloned.1.call-start = ((), (), s32[]{:S(2)}) async-start(), calls=%async_computation.15 | async-start | bytes 3981312 | tf_op jit(solution)/shard_map/reduce_scatter | solution.py:464
  443.6 27.0 %collective-permute-start.5 = (bf16[512,768]{0,1:T(8,128)(2,1)}, bf16[512,768]{0,1:T(8,128)(2,1)}, u32[]{:S(2)}, u32[]{:S(2)}) collective-permute-start(bf16[512,768]{0,1:T(8,128)(2,1)} %bitcast.45), channel_id=1, source_target_pairs={{2,0},{3,1},{4,2},{5,3},{6,4},{7,5},{10,8},{11,9},{12,10},{13,11},... | collective-permute-start | bytes 2359304 | tf_op jit(solution)/shard_map/ppermute | solution.py:27
  444.9 25.7 %collective-permute-start.4 = (bf16[512,768]{0,1:T(8,128)(2,1)}, bf16[512,768]{0,1:T(8,128)(2,1)}, u32[]{:S(2)}, u32[]{:S(2)}) collective-permute-start(bf16[512,768]{0,1:T(8,128)(2,1)} %bitcast.44), channel_id=1, source_target_pairs={{1,0},{2,1},{3,2},{4,3},{5,4},{6,5},{7,6},{9,8},{10,9},{11,10},{12... | collective-permute-start | bytes 2359304 | tf_op jit(solution)/shard_map/ppermute | solution.py:27
  456.7 46.3 %collective-permute-start.7 = (bf16[512,768]{0,1:T(8,128)(2,1)S(1)}, bf16[512,768]{0,1:T(8,128)(2,1)S(1)}, u32[]{:S(2)}, u32[]{:S(2)}) collective-permute-start(bf16[512,768]{0,1:T(8,128)(2,1)S(1)} %bitcast.202), channel_id=1, source_target_pairs={{2,0},{3,1},{4,2},{5,3},{6,4},{7,5},{10,8},{11,9},{12,10},{13,11},... | collective-permute-start | bytes 2359304 | tf_op jit(solution)/shard_map/ppermute | solution.py:27
  458.0 45.0 %collective-permute-start.6 = (bf16[512,768]{0,1:T(8,128)(2,1)S(1)}, bf16[512,768]{0,1:T(8,128)(2,1)S(1)}, u32[]{:S(2)}, u32[]{:S(2)}) collective-permute-start(bf16[512,768]{0,1:T(8,128)(2,1)S(1)} %bitcast.201), channel_id=1, source_target_pairs={{1,0},{2,1},{3,2},{4,3},{5,4},{6,5},{7,6},{9,8},{10,9},{11,10},{12... | collective-permute-start | bytes 2359304 | tf_op jit(solution)/shard_map/ppermute | solution.py:27
  509.2 102.0 %reduce-scatter.23.cloned.1.call-start = ((), (), s32[]{:S(2)}) async-start(), calls=%async_computation.20 | async-start | bytes 221184
  519.6 107.3 %reduce-scatter.21.cloned.1.call-start = ((), (), s32[]{:S(2)}) async-start(), calls=%async_computation.19 | async-start | bytes 221184
  520.9 137.2 %reduce-scatter.19.cloned.1.call-start = ((), (), s32[]{:S(2)}) async-start(), calls=%async_computation.18 | async-start | bytes 221184
  522.2 183.7 %all-reduce.14.cloned.1.call-start = ((), (), s32[]{:S(2)}) async-start(), calls=%async_computation.21 | async-start | bytes 1179648 | tf_op jit(solution)/shard_map/psum | solution.py:487
  563.9 243.8 %reduce-scatter.17.cloned.1.call-start = ((), (), s32[]{:S(2)}) async-start(), calls=%async_computation.17 | async-start | bytes 10616832 | tf_op jit(solution)/shard_map/reduce_scatter | solution.py:299
  570.9 88.0 %copy-start.26 = (bf16[512,768]{1,0:T(8,128)(2,1)S(1)}, bf16[512,768]{1,0:T(8,128)(2,1)}, u32[]{:S(2)}) copy-start(bf16[512,768]{1,0:T(8,128)(2,1)} %param.24) | copy-start | bytes 2359300
  570.9 88.0 %copy-start.32 = (bf16[512,3,12,64]{0,3,2,1:T(8,128)(2,1)S(1)}, bf16[512,3,12,64]{0,3,2,1:T(8,128)(2,1)}, u32[]{:S(2)}) copy-start(bf16[512,3,12,64]{0,3,2,1:T(8,128)(2,1)} %copy-done.31) | copy-start | bytes 7077892
  (75 other events, 903.7 us)
Sparse Core Ops, SparseCore 0:
  9.8 44.5 all-gather.8
  56.0 21.5 all-gather.10
  79.2 51.0 all-gather.14
  131.8 50.7 all-gather.16
  184.0 40.0 all-gather.12
  407.9 55.6 reduce-scatter.14
  509.3 54.5 reduce-scatter.12
  566.8 28.8 reduce-scatter.22
  598.5 28.4 reduce-scatter.20
  629.7 28.4 reduce-scatter.18
  661.2 44.7 all-reduce.13
  708.2 99.5 reduce-scatter.16
where the time goes:
time: 828 us; the launch traced here: 818 us
  waiting for transfers between devices  265 us (32%)
  matrix products  171 us (21%)
  other arithmetic  128 us (15%)
  blocking collectives  113 us (14%)
  local copies, waits for them, and re-layouts  90.1 us (11%)
  starting transfers between devices  33.8 us (4%)
  between operations  17.4 us (2%)
    reduce_scatter x1, waiting for transfers between devices, local(): lax.psum_scatter(jnp.concatenate([inward, outward], axis=1).astype(jnp.bf...  98.2 us
    ppermute x8, waiting for transfers between devices, shifted(): return lax.ppermute(array, axis, pairs)  63 us
    unnamed x15, waiting for transfers between devices  48.6 us
    reduce_scatter x1, waiting for transfers between devices, local(): lax.psum_scatter(projector_grad.astype(jnp.bfloat16), 'fsdp', scatter_dim...  37.9 us
    psum x1, blocking collectives, local(): gradient_carryover = lax.psum(carryover_local, ('expert', 'fsdp'))  37.9 us
    unnamed x2, blocking collectives  32.4 us
    dot_general x1, matrix products, local(): jnp.einsum('qhd,khd->hqk', attended_grad, value_all, preferred_element_ty...  27 us
    reduce_sum x1, other arithmetic, local(): gate_grad = jnp.sum(values_all * upstream[:, None, :], axis=2)  25.2 us
  transfers between devices with their start and end apart: 24, of which 10 were waited for; matrix products, arithmetic and copies ran while one was open for 28% of the time, Pallas kernels for 0%

commit v1 on v0

v1 whole, which is shorter than its diff:
```python
import functools
import math

import jax
import jax.numpy as jnp
from jax import lax
from jax.experimental import pallas as pl
from jax.experimental.pallas import tpu as pltpu
from jax.sharding import PartitionSpec as P

D = 768
H = 12
HD = 64
FF = 2048
WINDOW = 1024
CAP = 128

epsilon = 1e-06
rope_base = 10000.0
masked_score = -1e30
QTILE = 256
SPAN = QTILE + WINDOW
LANES = 128
PAIRS = H * HD // LANES
FTILE = 256
NT = (((1,), (1,)), ((), ()))
TN = (((0,), (0,)), ((), ()))
F32 = jnp.float32
BF16 = jnp.bfloat16
query_scale = 1.0 / math.sqrt(HD)


def vmem(megabytes):
    return pltpu.CompilerParams(vmem_limit_bytes=megabytes << 20)


def cost(flops, moved, trans=0):
    return pl.CostEstimate(flops=int(flops), bytes_accessed=int(moved), transcendentals=int(trans))


def dot(a, b):
    return jnp.dot(a, b, preferred_element_type=F32)


def dot_nt(a, b):
    return lax.dot_general(a, b, NT, preferred_element_type=F32)


def dot_tn(a, b):
    return lax.dot_general(a, b, TN, preferred_element_type=F32)


def halves(x):
    high = x.astype(BF16)
    return high, (x - high.astype(F32)).astype(BF16)


def lanes_of(shape):
    return lax.broadcasted_iota(jnp.int32, shape, len(shape) - 1)


def norm_scale(values):
    return lax.rsqrt(jnp.mean(values * values, axis=-1, keepdims=True) + epsilon)


def rope_tables(positions):
    lane = jnp.arange(LANES, dtype=jnp.int32)
    half = HD // 2
    freq_index = (lane % half).astype(F32)
    inverse = jnp.exp(freq_index * (-2.0 * math.log(rope_base) / HD))
    angles = positions[:, None] * inverse[None, :]
    sign = jnp.where(lane % HD < half, -1.0, 1.0).astype(F32)
    return jnp.cos(angles), jnp.sin(angles) * sign[None, :]


def swapped(x):
    half = HD // 2
    lane = lanes_of(x.shape)
    return jnp.where(
        lane % HD < half, pltpu.roll(x, LANES - half, 1), pltpu.roll(x, half, 1)
    )


def rotate(x, cosine, sine):
    return x * cosine + swapped(x) * sine


def rotate_back(x, cosine, sine):
    return x * cosine - swapped(x) * sine


def project_kernel(place, *refs):
    count = place.shape[0]
    chunks = refs[:count]
    tok_ref, cos_ref, sin_ref, w_ref, normed_ref, q_ref, k_ref, v_ref = refs[count:]
    rows = chunks[0].shape[0]
    step = pl.program_id(0)

    @pl.when(step == 0)
    def _():
        for i in range(count):
            at = pl.multiple_of(place[i] * rows, rows)
            w_ref[pl.ds(at, rows), :] = chunks[i][...]

    small = w_ref[:, 3 * D :].astype(F32).T
    gain = small[LANES - 2 : LANES - 1, :]
    x = tok_ref[...].astype(F32)
    normed = (x * norm_scale(x) * gain).astype(BF16)
    normed_ref[...] = normed
    cosine, sine = cos_ref[...], sin_ref[...]
    keys = dot(normed, w_ref[:, D : 2 * D])
    for j in range(PAIRS):
        part = slice(j * LANES, (j + 1) * LANES)
        k_ref[:, part] = rotate(keys[:, part], cosine, sine).astype(BF16)
    v_ref[...] = dot(normed, w_ref[:, 2 * D : 3 * D]).astype(BF16)

    @pl.when(step == pl.num_programs(0) - 1)
    def _():
        queries = dot(normed, w_ref[:, :D])
        for j in range(PAIRS):
            part = slice(j * LANES, (j + 1) * LANES)
            q_ref[:, part] = (rotate(queries[:, part], cosine, sine) * query_scale).astype(BF16)


def project(place, chunks, tokens_all, cosine, sine, tok):
    rows, width = chunks[0].shape
    blocks = tokens_all.shape[0] // tok
    fixed = lambda s, *_: (0, 0)
    moving = lambda s, *_: (s, 0)
    span = tokens_all.shape[0]
    return pl.pallas_call(
        project_kernel,
        grid_spec=pltpu.PrefetchScalarGridSpec(
            num_scalar_prefetch=1,
            grid=(blocks,),
            in_specs=[pl.BlockSpec((rows, width), fixed)] * len(chunks)
            + [
                pl.BlockSpec((tok, D), moving),
                pl.BlockSpec((tok, LANES), moving),
                pl.BlockSpec((tok, LANES), moving),
            ],
            out_specs=[
                pl.BlockSpec((D, width), fixed),
                pl.BlockSpec((tok, D), moving),
                pl.BlockSpec((tok, D), fixed),
                pl.BlockSpec((tok, D), moving),
                pl.BlockSpec((tok, D), moving),
            ],
        ),
        out_shape=[
            jax.ShapeDtypeStruct((D, width), BF16),
            jax.ShapeDtypeStruct((span, D), BF16),
            jax.ShapeDtypeStruct((tok, D), BF16),
            jax.ShapeDtypeStruct((span, D), BF16),
            jax.ShapeDtypeStruct((span, D), BF16),
        ],
        compiler_params=vmem(56),
        cost_estimate=cost(2 * span * D * 2 * D, 20 << 20),
        name="project",
    )(place, *chunks, tokens_all, cosine, sine)


def head_mask(x, head):
    return jnp.where(lanes_of(x.shape) // HD == head, x, jnp.zeros_like(x))


def attend_kernel(q_ref, k_ref, v_ref, bias_ref, o_ref, lse_ref, vt_ref):
    vt_ref[...] = v_ref[...].T
    for t in range(q_ref.shape[0] // QTILE):
        rows = slice(t * QTILE, (t + 1) * QTILE)
        span = slice(t * QTILE, t * QTILE + SPAN)
        keys, queries = k_ref[span, :], q_ref[rows, :]
        parts = []
        for h in range(2):
            s = dot_nt(keys, head_mask(queries, h)) + bias_ref[t]
            top = jnp.max(s, axis=0, keepdims=True)
            e = jnp.exp(s - top)
            total = jnp.sum(e, axis=0, keepdims=True)
            o = dot(vt_ref[h * HD : (h + 1) * HD, span], e.astype(BF16))
            parts.append(o / total)
            lse_ref[0, h : h + 1, rows] = top + jnp.log(total)
        o_ref[rows, :] = jnp.concatenate(parts, axis=0).T.astype(BF16)


def attend(q, k, v, bias):
    tok, span = q.shape[0], k.shape[0]
    col = lambda p: (0, p)
    return pl.pallas_call(
        attend_kernel,
        grid=(PAIRS,),
        in_specs=[
            pl.BlockSpec((tok, LANES), col),
            pl.BlockSpec((span, LANES), col),
            pl.BlockSpec((span, LANES), col),
            pl.BlockSpec(bias.shape, lambda p: (0, 0, 0)),
        ],
        out_specs=[
            pl.BlockSpec((tok, LANES), col),
            pl.BlockSpec((1, 8, tok), lambda p: (p, 0, 0)),
        ],
        out_shape=[
            jax.ShapeDtypeStruct((tok, D), BF16),
            jax.ShapeDtypeStruct((PAIRS, 8, tok), F32),
        ],
        scratch_shapes=[pltpu.VMEM((LANES, span), BF16)],
        compiler_params=vmem(56),
        cost_estimate=cost(4 * tok * SPAN * D * 4, 10 << 20, tok * SPAN * H),
        name="attend",
    )(q, k, v, bias)


def attend_back_kernel(
    q_ref, k_ref, v_ref, o_ref, do_ref, lse_ref, bias_ref, cos_ref, sin_ref,
    dq_ref, dk_ref, dv_ref, kt_ref, dk_sum, dv_sum,
):
    tok = q_ref.shape[0]
    own = k_ref.shape[0] - tok
    kt_ref[...] = k_ref[...].T
    dk_sum[...] = jnp.zeros_like(dk_sum)
    dv_sum[...] = jnp.zeros_like(dv_sum)
    for t in range(tok // QTILE):
        rows = slice(t * QTILE, (t + 1) * QTILE)
        span = slice(t * QTILE, t * QTILE + SPAN)
        keys, values = k_ref[span, :], v_ref[span, :]
        queries, upstream = q_ref[rows, :], do_ref[rows, :]
        product = (upstream.astype(F32) * o_ref[rows, :].astype(F32)).T
        dq_parts = []
        for h in range(2):
            head = slice(h * HD, (h + 1) * HD)
            qh, gh = head_mask(queries, h), head_mask(upstream, h)
            s = dot_nt(keys, qh) + bias_ref[t]
            p = jnp.exp(s - lse_ref[0, h : h + 1, rows])
            dp = dot_nt(values, gh)
            delta = jnp.sum(product[head, :], axis=0, keepdims=True)
            ds = (p * (dp - delta)).astype(BF16)
            dv_sum[span, :] += dot(p.astype(BF16), gh)
            dk_sum[span, :] += dot(ds, qh)
            dq_parts.append(dot(kt_ref[head, span], ds))
        dq = jnp.concatenate(dq_parts, axis=0).T
        there = slice(own + t * QTILE, own + (t + 1) * QTILE)
        dq = rotate_back(dq, cos_ref[there, :], sin_ref[there, :]) * query_scale
        dq_ref[rows, :] = dq.astype(BF16)
    dk_ref[...] = rotate_back(dk_sum[...], cos_ref[...], sin_ref[...]).astype(BF16)
    dv_ref[...] = dv_sum[...].astype(BF16)


def attend_back(q, k, v, o, do, lse, bias, cosine, sine):
    tok, span = q.shape[0], k.shape[0]
    col = lambda p: (0, p)
    whole = lambda p: (0, 0)
    mine = pl.BlockSpec((tok, LANES), col)
    long = pl.BlockSpec((span, LANES), col)
    return pl.pallas_call(
        attend_back_kernel,
        grid=(PAIRS,),
        in_specs=[
            mine,
            long,
            long,
            mine,
            mine,
            pl.BlockSpec((1, 8, tok), lambda p: (p, 0, 0)),
            pl.BlockSpec(bias.shape, lambda p: (0, 0, 0)),
            pl.BlockSpec((span, LANES), whole),
            pl.BlockSpec((span, LANES), whole),
        ],
        out_specs=[mine, long, long],
        out_shape=[
            jax.ShapeDtypeStruct((tok, D), BF16),
            jax.ShapeDtypeStruct((span, D), BF16),
            jax.ShapeDtypeStruct((span, D), BF16),
        ],
        scratch_shapes=[
            pltpu.VMEM((LANES, span), BF16),
            pltpu.VMEM((span, LANES), F32),
            pltpu.VMEM((span, LANES), F32),
        ],
        compiler_params=vmem(56),
        cost_estimate=cost(10 * tok * SPAN * D * 4, 20 << 20, tok * SPAN * H),
        name="attend_back",
    )(q, k, v, o, do, lse, bias, cosine, sine)


def route_kernel(
    experts, att_ref, col_ref, tok_ref, cot_ref, small_ref, past_ref, routes_ref, slots_ref,
    residual_ref, hidden_ref, aux_ref, send_ref,
):
    small = small_ref[...]
    gain = small.astype(F32).T[LANES - 1 : LANES, :]
    residual = tok_ref[...].astype(F32) + dot(att_ref[...], col_ref[...])
    scale = norm_scale(residual)
    hidden = (residual * scale * gain).astype(BF16)
    residual_ref[...] = residual
    hidden_ref[...] = hidden
    mixed = dot(hidden, small)
    logits = mixed + past_ref[...]
    lane = lanes_of(logits.shape)
    routes = routes_ref[...]
    picked = [
        jnp.sum(jnp.where(lane == routes[:, k : k + 1], logits, 0.0), axis=1, keepdims=True)
        for k in range(2)
    ]
    top = jnp.maximum(picked[0], picked[1])
    raised = [jnp.exp(x - top) for x in picked]
    total = raised[0] + raised[1]
    gates = [x / total for x in raised]
    names = experts + 4
    aux = [gates[0], gates[1]]
    for c in range(2):
        pair = [mixed[:, names + 2 * c + i : names + 2 * c + i + 1] for i in range(2)]
        above = jnp.maximum(pair[0], pair[1])
        up = [jnp.exp(x - above) for x in pair]
        aux += [up[0] / (up[0] + up[1]), up[1] / (up[0] + up[1])]
    aux.append(scale)
    packed = jnp.zeros(logits.shape, F32)
    for i, value in enumerate(aux):
        packed = jnp.where(lane == i, value, packed)
    aux_ref[...] = packed
    cot = cot_ref[...].astype(F32)
    slots = slots_ref[...]
    count, tok = send_ref.shape[0], hidden.shape[0]
    where = lax.broadcasted_iota(jnp.int32, (count, tok), 0)
    hot = [(where == slots[k : k + 1, :]).astype(F32).astype(BF16) for k in range(2)]
    send_ref[:, :D] = dot(hot[0] + hot[1], hidden).astype(BF16)
    grads = dot(hot[0], (gates[0] * cot).astype(BF16)) + dot(hot[1], (gates[1] * cot).astype(BF16))
    send_ref[:, D:] = grads.astype(BF16)


def whole_specs(arrays):
    return [pl.BlockSpec(memory_space=pltpu.VMEM) for _ in arrays]


def route(experts, *args):
    tok = args[0].shape[0]
    outs = [
        jax.ShapeDtypeStruct((tok, D), F32),
        jax.ShapeDtypeStruct((tok, D), BF16),
        jax.ShapeDtypeStruct((tok, LANES), F32),
        jax.ShapeDtypeStruct((experts * CAP, 2 * D), BF16),
    ]
    return pl.pallas_call(
        functools.partial(route_kernel, experts),
        in_specs=whole_specs(args),
        out_specs=whole_specs(outs),
        out_shape=outs,
        compiler_params=vmem(56),
        cost_estimate=cost(2 * tok * D * (D + 3 * experts * CAP), 9 << 20),
        name="route",
    )(*args)


def expert_kernel(x_ref, gw_ref, uw_ref, dw_ref, out_ref, low_ref, answer, back):
    step = pl.program_id(0)

    @pl.when(step == 0)
    def _():
        answer[...] = jnp.zeros_like(answer)
        back[...] = jnp.zeros_like(back)

    rows, grads = x_ref[:, :D], x_ref[:, D:]
    gw, uw, dw = gw_ref[...], uw_ref[...], dw_ref[...]
    pre = dot(rows, gw)
    up = dot(rows, uw)
    grad = dot(grads, dw)
    sigmoid = 1.0 / (1.0 + jnp.exp(-pre))
    active = pre * sigmoid
    hidden = (active * up).astype(BF16)
    gate_low = (grad * up * sigmoid * (1.0 + pre * (1.0 - sigmoid))).astype(BF16)
    up_low = (grad * active).astype(BF16)
    low_ref[0] = gate_low
    low_ref[1] = up_low
    low_ref[2] = hidden
    answer[...] += dot_nt(hidden, dw)
    back[...] += dot_nt(gate_low, gw) + dot_nt(up_low, uw)

    @pl.when(step == pl.num_programs(0) - 1)
    def _():
        out_ref[:, :D] = answer[...].astype(BF16)
        out_ref[:, D:] = back[...].astype(BF16)


def expert_rows(x, gating, upward, downward):
    rows = x.shape[0]
    weight = pl.BlockSpec((D, FTILE), lambda j: (0, j))
    return pl.pallas_call(
        expert_kernel,
        grid=(FF // FTILE,),
        in_specs=[pl.BlockSpec((rows, 2 * D), lambda j: (0, 0)), weight, weight, weight],
        out_specs=[
            pl.BlockSpec((rows, 2 * D), lambda j: (0, 0)),
            pl.BlockSpec((3, rows, FTILE), lambda j: (0, 0, j)),
        ],
        out_shape=[
            jax.ShapeDtypeStruct((rows, 2 * D), BF16),
            jax.ShapeDtypeStruct((3, rows, FF), BF16),
        ],
        scratch_shapes=[pltpu.VMEM((rows, D), F32), pltpu.VMEM((rows, D), F32)],
        compiler_params=vmem(56),
        cost_estimate=cost(12 * rows * D * FF, 20 << 20),
        name="expert_rows",
    )(x, gating, upward, downward)


def expert_sums_kernel(x_ref, low_ref, out_ref, turned):
    step = pl.program_id(0)
    tiles = FF // FTILE

    @pl.when(step == 0)
    def _():
        turned[...] = x_ref[:, :D].T

    @pl.when(step == 2 * tiles)
    def _():
        turned[...] = x_ref[:, D:].T

    out_ref[...] = dot(turned[...], low_ref[0]).astype(BF16)


def expert_sums(x, low):
    rows = x.shape[0]
    tiles = FF // FTILE
    return pl.pallas_call(
        expert_sums_kernel,
        grid=(3 * tiles,),
        in_specs=[
            pl.BlockSpec((rows, 2 * D), lambda j: (0, 0)),
            pl.BlockSpec((1, rows, FTILE), lambda j: (j // tiles, 0, j % tiles)),
        ],
        out_specs=pl.BlockSpec((D, FTILE), lambda j: (0, j)),
        out_shape=jax.ShapeDtypeStruct((D, 3 * FF), BF16),
        scratch_shapes=[pltpu.VMEM((D, rows), BF16)],
        compiler_params=vmem(56),
        cost_estimate=cost(6 * rows * D * FF, 20 << 20),
        name="expert_sums",
    )(x, low)


def combine_kernel(
    experts, back_ref, residual_ref, hidden_ref, cot_ref, aux_ref, small_ref, col_ref, att_ref,
    past_ref, carry_ref, routes_ref, slots_ref,
    layer_ref, rgrad_ref, agrad_ref, logits_ref, colgrad_ref, smallgrad_ref, carrygrad_ref,
):
    tok = hidden_ref.shape[0]
    names = experts + 4
    slots, routes = slots_ref[...], routes_ref[...]
    count = back_ref.shape[0]
    where = lax.broadcasted_iota(jnp.int32, (tok, count), 1)
    hot = [(where == slots[:, k : k + 1]).astype(F32).astype(BF16) for k in range(2)]
    answers, returned = back_ref[:, :D], back_ref[:, D:]
    values = [dot(hot[k], answers) for k in range(2)]
    hidden_grad = dot(hot[0] + hot[1], returned)
    hidden_low, cot_low = hidden_ref[...], cot_ref[...]
    hidden, cot = hidden_low.astype(F32), cot_low.astype(F32)
    residual = residual_ref[...]
    small = small_ref[...]
    turned = small.astype(F32).T
    aux = aux_ref[...]
    gates = [aux[:, k : k + 1] for k in range(2)]
    mixing = [[aux[:, 2 + 2 * c + i : 3 + 2 * c + i] for i in range(2)] for c in range(2)]
    scale = aux[:, 6:7]
    both = jnp.sum(hidden * cot, axis=1, keepdims=True)
    against = dot(cot_low, small)
    fixed = [against[:, names + 4 + c : names + 5 + c] for c in range(2)]
    constant = [turned[names + 4 + c : names + 5 + c, :] for c in range(2)]

    def on(k, e):
        return (routes[:, k : k + 1] == e).astype(F32)

    gate_grad = []
    for k in range(2):
        total = jnp.sum(values[k] * cot, axis=1, keepdims=True) + on(k, experts + 1) * both
        for c in range(2):
            total += on(k, experts + 2 + c) * (mixing[c][0] * both + mixing[c][1] * fixed[c])
        gate_grad.append(total)
    mean = gates[0] * gate_grad[0] + gates[1] * gate_grad[1]
    chosen = [gates[k] * (gate_grad[k] - mean) for k in range(2)]
    weight = [sum(on(k, experts + 2 + c) * gates[k] for k in range(2)) for c in range(2)]
    copied = sum(on(k, experts + 1) * gates[k] for k in range(2))
    copied += weight[0] * mixing[0][0] + weight[1] * mixing[1][0]
    lane = lanes_of((tok, LANES))
    logit_grad = jnp.where(lane == routes[:, 0:1], chosen[0], 0.0)
    logit_grad += jnp.where(lane == routes[:, 1:2], chosen[1], 0.0)
    wide = logit_grad
    shares = jnp.zeros((tok, LANES), F32)
    output = residual + gates[0] * values[0] + gates[1] * values[1] + copied * hidden
    for c in range(2):
        parts = [weight[c] * both, weight[c] * fixed[c]]
        middle = mixing[c][0] * parts[0] + mixing[c][1] * parts[1]
        for i in range(2):
            wide = jnp.where(lane == names + 2 * c + i, mixing[c][i] * (parts[i] - middle), wide)
        share = weight[c] * mixing[c][1]
        shares = jnp.where(lane == names + 4 + c, share, shares)
        output += share * constant[c]
    layer_ref[...] = output.astype(BF16)
    logits_ref[...] = lax.dot_general(
        logit_grad, carry_ref[...], NT, precision=lax.Precision.HIGHEST,
        preferred_element_type=F32,
    )
    carrygrad_ref[...] = lax.dot_general(
        past_ref[...], logit_grad, TN, precision=lax.Precision.HIGHEST,
        preferred_element_type=F32,
    )
    high, low = halves(wide)
    hidden_grad += copied * cot + dot_nt(high, small) + dot_nt(low, small)
    scaled = hidden_grad * turned[LANES - 1 : LANES, :]
    residual_grad = (
        cot
        + scale * scaled
        - residual * (scale * scale * scale) * jnp.mean(scaled * residual, axis=1, keepdims=True)
    )
    rgrad_ref[...] = residual_grad
    residual_low = residual_grad.astype(BF16)
    agrad_ref[...] = dot_nt(residual_low, col_ref[...]).astype(BF16)
    colgrad_ref[...] = dot_tn(att_ref[...], residual_low).astype(BF16)
    gained = jnp.sum((hidden_grad * residual * scale).reshape(tok // 8, 8, D), axis=0)
    gained = jnp.sum(gained, axis=0, keepdims=True)
    column = lax.broadcasted_iota(jnp.int32, (LANES, D), 0)
    second = jnp.where(column == LANES - 1, gained, 0.0).T
    shares_high, shares_low = halves(shares)
    smallgrad_ref[...] = (
        second
        + dot_tn(hidden_low, high)
        + dot_tn(hidden_low, low)
        + dot_tn(cot_low, shares_high)
        + dot_tn(cot_low, shares_low)
    )


def combine(experts, *args):
    tok = args[1].shape[0]
    outs = [
        jax.ShapeDtypeStruct((tok, D), BF16),
        jax.ShapeDtypeStruct((tok, D), F32),
        jax.ShapeDtypeStruct((tok, D), BF16),
        jax.ShapeDtypeStruct((tok, LANES), F32),
        jax.ShapeDtypeStruct((D, D), BF16),
        jax.ShapeDtypeStruct((D, LANES), F32),
        jax.ShapeDtypeStruct((LANES, LANES), F32),
    ]
    return pl.pallas_call(
        functools.partial(combine_kernel, experts),
        in_specs=whole_specs(args),
        out_specs=whole_specs(outs),
        out_shape=outs,
        compiler_params=vmem(56),
        cost_estimate=cost(2 * tok * D * (2 * D + 3 * experts * CAP), 14 << 20),
        name="combine",
    )(*args)


def normed_grad_kernel(dq_ref, dk_ref, dv_ref, tok_ref, w_ref, halo_ref, own_ref, first_ref):
    step = pl.program_id(0)
    last = pl.num_programs(0) - 1

    @pl.when(step == 0)
    def _():
        first_ref[...] = jnp.zeros_like(first_ref)

    x = tok_ref[...].astype(F32)
    weight = x * norm_scale(x)

    def add(grad):
        rows = grad.shape[0]
        first_ref[...] += jnp.sum((grad * weight).reshape(rows // 8, 8, D), axis=0)

    grad = dot_nt(dk_ref[...], w_ref[:, D : 2 * D]) + dot_nt(dv_ref[...], w_ref[:, 2 * D : 3 * D])

    @pl.when(step < last)
    def _():
        halo_ref[...] = grad.astype(BF16)
        add(grad)

    @pl.when(step == last)
    def _():
        full = grad + dot_nt(dq_ref[...], w_ref[:, :D])
        own_ref[...] = full
        add(full)


def normed_grad(dq, dk, dv, tokens_all, weights):
    tok, span = dq.shape[0], dk.shape[0]
    blocks = span // tok
    fixed = lambda s: (0, 0)
    moving = lambda s: (s, 0)
    return pl.pallas_call(
        normed_grad_kernel,
        grid=(blocks,),
        in_specs=[
            pl.BlockSpec((tok, D), fixed),
            pl.BlockSpec((tok, D), moving),
            pl.BlockSpec((tok, D), moving),
            pl.BlockSpec((tok, D), moving),
            pl.BlockSpec(weights.shape, fixed),
        ],
        out_specs=[
            pl.BlockSpec((tok, D), lambda s: (jnp.minimum(s, blocks - 2), 0)),
            pl.BlockSpec((tok, D), fixed),
            pl.BlockSpec((8, D), fixed),
        ],
        out_shape=[
            jax.ShapeDtypeStruct((span - tok, D), BF16),
            jax.ShapeDtypeStruct((tok, D), F32),
            jax.ShapeDtypeStruct((8, D), F32),
        ],
        compiler_params=vmem(56),
        cost_estimate=cost(4 * span * D * D, 16 << 20),
        name="normed_grad",
    )(dq, dk, dv, tokens_all, weights)


def project_grad_kernel(normed_ref, dq_ref, dk_ref, dv_ref, first_ref, out_ref, turned):
    tok = dq_ref.shape[0]
    own = normed_ref.shape[0] - tok
    step = pl.program_id(0)
    tiles = D // FTILE

    @pl.when(step == 0)
    def _():
        turned[...] = normed_ref[...].T

    @pl.when(step < tiles)
    def _():
        out_ref[...] = dot(turned[:, own:], dq_ref[...]).astype(BF16)

    @pl.when((step >= tiles) & (step < 2 * tiles))
    def _():
        out_ref[...] = dot(turned[...], dk_ref[...]).astype(BF16)

    @pl.when((step >= 2 * tiles) & (step < 3 * tiles))
    def _():
        out_ref[...] = dot(turned[...], dv_ref[...]).astype(BF16)

    @pl.when(step == 3 * tiles)
    def _():
        total = jnp.sum(first_ref[...], axis=0, keepdims=True)
        column = lax.broadcasted_iota(jnp.int32, (FTILE, D), 0)
        out_ref[...] = jnp.where(column == 0, total, 0.0).T.astype(BF16)


def project_grad(normed_all, dq, dk, dv, first):
    tok, span = dq.shape[0], dk.shape[0]
    tiles = D // FTILE
    fixed = lambda s: (0, 0)

    def tile(base):
        return lambda s: (0, jnp.clip(s - base, 0, tiles - 1))

    return pl.pallas_call(
        project_grad_kernel,
        grid=(3 * tiles + 1,),
        in_specs=[
            pl.BlockSpec((span, D), fixed),
            pl.BlockSpec((tok, FTILE), tile(0)),
            pl.BlockSpec((span, FTILE), tile(tiles)),
            pl.BlockSpec((span, FTILE), tile(2 * tiles)),
            pl.BlockSpec((8, D), fixed),
        ],
        out_specs=pl.BlockSpec((D, FTILE), lambda s: (0, s)),
        out_shape=jax.ShapeDtypeStruct((D, 3 * D + FTILE), BF16),
        scratch_shapes=[pltpu.VMEM((D, span), BF16)],
        compiler_params=vmem(56),
        cost_estimate=cost(4 * span * D * D, 12 << 20),
        name="project_grad",
    )(normed_all, dq, dk, dv, first)


def folded(count):
    return [0] + list(range(1, count, 2)) + list(range(2, count, 2))[::-1]


def siblings(count):
    return [(i, i ^ 1) for i in range(count)]


def ring_gather(x, count):
    chips = count // 2
    order = folded(chips)
    follow = {order[i]: order[(i + 1) % chips] for i in range(chips)}
    pairs = [(2 * z + c, 2 * follow[z] + c) for z in range(chips) for c in range(2)]
    me = lax.axis_index("fsdp")
    chip, core = me // 2, me % 2
    at = jnp.array([order.index(z) for z in range(chips)], jnp.int32)[chip]
    ring = jnp.array(order, jnp.int32)
    chunks, places = [], []
    current = x
    for k in range(chips):
        source = ring[(at - k) % chips]
        chunks += [current, lax.ppermute(current, "fsdp", siblings(count))]
        places += [2 * source + core, 2 * source + 1 - core]
        if k + 1 < chips:
            current = lax.ppermute(current, "fsdp", pairs)
    return chunks, jnp.stack(places).astype(jnp.int32)


def earlier_rows(x, count):
    up = [(i, i + 2) for i in range(count - 2)]
    second = lax.ppermute(x, "fsdp", up)
    core = lax.axis_index("fsdp") % 2
    first = lax.ppermute(jnp.where(core == 0, x, second), "fsdp", siblings(count))
    return second, first


def return_rows(second, first, own, count):
    down = [(i + 2, i) for i in range(count - 2)]
    core = lax.axis_index("fsdp") % 2
    across = lax.ppermute(first, "fsdp", siblings(count)).astype(F32)
    total = jnp.where(core == 0, second.astype(F32), second.astype(F32) + across)
    after = lax.ppermute(total.astype(BF16), "fsdp", down).astype(F32)
    return own + after + jnp.where(core == 0, across, 0.0)


def reduce_rows(x, experts, count):
    chips = count // 2
    rows, width = x.shape
    piece = rows // (count * experts)
    core = lax.axis_index("fsdp") % 2
    x = x.reshape(chips, 2, experts, piece, width)
    mine = lax.dynamic_index_in_dim(x, core, 1, False)
    theirs = lax.dynamic_index_in_dim(x, 1 - core, 1, False)
    other = lax.ppermute(theirs, "fsdp", siblings(count))
    x = (mine.astype(F32) + other.astype(F32)).astype(BF16)
    x = x.transpose(1, 0, 2, 3).reshape(experts, chips * piece, width)
    x = lax.all_to_all(x, "expert", split_axis=0, concat_axis=0, tiled=True)
    x = jnp.sum(x.astype(F32), axis=0).astype(BF16).reshape(chips, piece, width)
    groups = [[2 * z + c for z in range(chips)] for c in range(2)]
    x = lax.all_to_all(
        x, "fsdp", split_axis=0, concat_axis=0, tiled=True, axis_index_groups=groups
    )
    x = jnp.sum(x.astype(F32), axis=0)
    return lax.all_gather(x.astype(BF16), "expert", axis=0, tiled=True).astype(F32), x


def local(
    tokens,
    past_logits,
    routes,
    lengths,
    projector,
    collector,
    router,
    blender,
    constants,
    first_gain,
    second_gain,
    carryover,
    gating,
    upward,
    downward,
    cotangent,
):
    tok = tokens.shape[0]
    experts = lax.axis_size("expert")
    count = lax.axis_size("fsdp")
    names = experts + 4
    hops = WINDOW // tok
    me = lax.axis_index("fsdp")

    shard = projector.shape[0]
    gap = LANES - names - 8
    small = jnp.concatenate(
        [router, blender, constants, jnp.zeros((shard, gap), BF16)]
        + [first_gain[:, None], second_gain[:, None]],
        axis=1,
    )
    chunks, places = ring_gather(jnp.concatenate([projector, small], axis=1), count)
    second, first = earlier_rows(tokens, count)
    tokens_all = jnp.concatenate([second, first, tokens], axis=0)
    collector_all = lax.all_gather(collector, "fsdp", axis=0, tiled=True)
    gating_all = lax.all_gather(gating[0], "fsdp", axis=0, tiled=True)
    upward_all = lax.all_gather(upward[0], "fsdp", axis=0, tiled=True)
    downward_all = lax.all_gather(downward[0], "fsdp", axis=0, tiled=True)

    span = tok + WINDOW
    key_positions = (me - hops) * tok + jnp.arange(span, dtype=jnp.int32)
    cosine, sine = rope_tables(key_positions.astype(F32))
    bounds = jnp.cumsum(lengths[0])
    biases = []
    for t in range(tok // QTILE):
        at = me * tok + t * QTILE + jnp.arange(QTILE, dtype=jnp.int32)
        start = jnp.max(jnp.where(bounds[:, None] <= at[None, :], bounds[:, None], 0), axis=0)
        least = jnp.maximum(at - (WINDOW - 1), start)
        keys_at = key_positions[t * QTILE : t * QTILE + SPAN, None]
        inside = (keys_at >= least[None, :]) & (keys_at <= at[None, :])
        biases.append(jnp.where(inside, 0.0, masked_score).astype(F32))
    bias = jnp.stack(biases)
    onehot = (routes[:, :, None] == jnp.arange(experts, dtype=jnp.int32)).astype(BF16)
    per_token = jnp.sum(onehot, axis=1)
    lower = jnp.tril(jnp.ones((tok, tok), BF16), -1)
    before = jnp.dot(lower, per_token, preferred_element_type=F32)
    position_in = jnp.sum(onehot.astype(F32) * before[:, None, :], axis=2).astype(jnp.int32)
    slots = jnp.where(routes < experts, routes * CAP + position_in, experts * CAP)
    past_part = jnp.dot(
        past_logits, carryover, precision=lax.Precision.HIGHEST, preferred_element_type=F32
    )
    past_part = jnp.pad(past_part, ((0, 0), (0, LANES - names)))
    past_wide = jnp.pad(past_logits, ((0, 0), (0, LANES - names)))
    carry_wide = jnp.pad(carryover, ((0, LANES - names), (0, LANES - names)))

    weights, normed_all, q, k, v = project(places, chunks, tokens_all, cosine, sine, tok)
    small_all = weights[:, 3 * D :]
    attended, lse = attend(q, k, v, bias)
    residual, hidden, aux, send = route(
        experts, attended, collector_all, tokens, cotangent, small_all, past_part, routes, slots.T
    )

    def exchange(x):
        x = x.reshape(experts, CAP, 2 * D)
        x = lax.all_to_all(x, "expert", split_axis=0, concat_axis=0, tiled=True)
        return x.reshape(experts * CAP, 2 * D)

    arrived = exchange(send)
    answers, low = expert_rows(arrived, gating_all, upward_all, downward_all)
    returned = exchange(answers)
    sums = expert_sums(arrived, low)
    sums = lax.psum_scatter(sums, "fsdp", scatter_dimension=0, tiled=True).astype(F32)

    layer_output, residual_grad, attended_grad, logits_grad, col_grad, small_grad, carry_grad = (
        combine(
            experts, returned, residual, hidden, cotangent, aux, small_all, collector_all,
            attended, past_wide, carry_wide, routes, slots,
        )
    )
    piece = D // (count * experts)
    wide = -(-names * names // piece)
    flat = jnp.pad(carry_grad[:names, :names].reshape(-1), (0, piece * wide - names * names))
    ride = jnp.tile(flat.reshape(piece, wide), (count * experts, 1))
    small_grad = jnp.concatenate(
        [small_grad[:, : names + 6], ride, small_grad[:, names + 6 + wide :]], axis=1
    )
    col_rows, col_piece = reduce_rows(
        jnp.concatenate([col_grad, small_grad.astype(BF16)], axis=1), experts, count
    )
    dq, dk, dv = attend_back(q, k, v, attended, attended_grad, lse, bias, cosine, sine)
    halo_grad, own_grad, first_sum = normed_grad(dq, dk, dv, tokens_all, weights)
    projector_grad = project_grad(normed_all, dq, dk, dv, first_sum)
    own_grad = return_rows(halo_grad[:tok], halo_grad[tok:], own_grad, count)
    projector_rows, _ = reduce_rows(projector_grad, experts, count)

    tokens_wide = tokens.astype(F32)
    first_scale = norm_scale(tokens_wide)
    scaled = own_grad * weights[:, 3 * D + LANES - 2].astype(F32)
    gradient_tokens = (
        residual_grad
        + first_scale * scaled
        - tokens_wide
        * (first_scale * first_scale * first_scale)
        * jnp.mean(scaled * tokens_wide, axis=-1, keepdims=True)
    ).astype(BF16)
    ridden = col_piece[:, D + names + 6 : D + names + 6 + wide].reshape(-1)
    return (
        layer_output,
        gradient_tokens,
        logits_grad[:, :names],
        projector_rows[:, : 3 * D],
        col_rows[:, :D],
        col_rows[:, D : D + names],
        col_rows[:, D + names : D + names + 4],
        col_rows[:, D + names + 4 : D + names + 6],
        projector_rows[:, 3 * D],
        col_rows[:, D + LANES - 1],
        ridden[: names * names].reshape(names, names),
        sums[:, :FF][None],
        sums[:, FF : 2 * FF][None],
        sums[:, 2 * FF :][None],
    )


def solution(mesh):
    rows = P(("expert", "fsdp"), None)
    shared = P("fsdp", None)
    expert = P("expert", "fsdp", None)
    return jax.shard_map(
        local,
        mesh=mesh,
        in_specs=(
            rows, rows, rows, P("expert", None), shared, shared, shared, shared, shared,
            P("fsdp"), P("fsdp"), P(), expert, expert, expert, rows,
        ),
        out_specs=(
            rows, rows, rows, shared, shared, shared, shared, shared,
            P("fsdp"), P("fsdp"), P(), expert, expert, expert,
        ),
        check_vma=False,
    )
```

time: 828 us -> 423 us (0.51)
  waiting for transfers between devices: 265 us -> 83.2 us
  matrix products: 171 us -> 1.62 us
  Pallas kernels: 0 us -> 142 us
  other arithmetic: 128 us -> 29.4 us
  blocking collectives: 113 us -> 53.4 us
  local copies, waits for them, and re-layouts: 90.1 us -> 41.4 us
  starting transfers between devices: 33.8 us -> 45.7 us
    dot_general x29 -> x2, matrix products: 171 us -> 1.62 us  [the longest x1 1.3 us: local(): jnp.dot(past_logits, carryover, precision=lax.Precision.HIGHEST, preferre...]
    pallas_call x0 -> x9, Pallas kernels: none -> 142 us  [the longest x1 25.4 us: attend_back(): pl.pallas_call(attend_back_kernel, grid=(PAIRS,), in_specs=[mine, long, l...]
    reduce_scatter x3 -> x1, waiting for transfers between devices: 136 us -> 0.01 us  [local(): lax.psum_scatter(sums, 'fsdp', scatter_dimension=0, tiled=True).astype(F32)]
    reduce_sum x12 -> x5, other arithmetic: 62.4 us -> 3.04 us  [the longest x2 1.99 us: reduce_rows(): x = jnp.sum(x.astype(F32), axis=0).astype(BF16).reshape(chips, piece, width)]
    psum x2 -> x0, blocking collectives: 48.1 us -> none  [the longest x1 37.9 us: local(): gradient_carryover = lax.psum(carryover_local, ('expert', 'fsdp'))]
    unnamed x15 -> x5, waiting for transfers between devices: 48.6 us -> 2.09 us
    unnamed x2 -> x0, blocking collectives: 32.4 us -> none
    all_to_all x4 -> x5, waiting for transfers between devices: 5.63 us -> 37.8 us  [the longest x1 18.3 us: exchange(): x = lax.all_to_all(x, 'expert', split_axis=0, concat_axis=0, tiled=True)]
  transfers between devices with their start and end apart: 24 -> 23, of which waited for: 10 -> 10; matrix products, arithmetic and copies ran while one was open for 28% -> 16% of each run, Pallas kernels for 0% -> 25%
where the time goes in v1:
time: 423 us; the launch traced here: 418 us
  Pallas kernels  142 us (34%)
  waiting for transfers between devices  83.2 us (20%)
  blocking collectives  53.4 us (13%)
  starting transfers between devices  45.7 us (11%)
  local copies, waits for them, and re-layouts  41.4 us (10%)
  other arithmetic  29.4 us (7%)
  between operations  21.3 us (5%)
    ppermute x3, waiting for transfers between devices, ring_gather(): current = lax.ppermute(current, 'fsdp', pairs)  37.1 us
    all_gather x2, blocking collectives, reduce_rows(): lax.all_gather(x.astype(BF16), 'expert', axis=0, tiled=True).astype(F32)  28 us
    pallas_call x1, Pallas kernels, attend_back(): pl.pallas_call(attend_back_kernel, grid=(PAIRS,), in_specs=[mine, long, l...  25.4 us
    all_to_all x1, blocking collectives, exchange(): x = lax.all_to_all(x, 'expert', split_axis=0, concat_axis=0, tiled=True)  25.3 us
    pallas_call x1, Pallas kernels, attend(): pl.pallas_call(attend_kernel, grid=(PAIRS,), in_specs=[pl.BlockSpec((tok,...  24.2 us
    pallas_call x1, Pallas kernels, expert_sums(): pl.pallas_call(expert_sums_kernel, grid=(3 * tiles,), in_specs=[pl.BlockS...  20.2 us
    ppermute x3, starting transfers between devices, ring_gather(): current = lax.ppermute(current, 'fsdp', pairs)  19 us
    all_to_all x1, waiting for transfers between devices, exchange(): x = lax.all_to_all(x, 'expert', split_axis=0, concat_axis=0, tiled=True)  18.3 us
  transfers between devices with their start and end apart: 23, of which 10 were waited for; matrix products, arithmetic and copies ran while one was open for 16% of the time, Pallas kernels for 25%

profile of v1, /device:TPU:0, one launch (start us, length us, event | category | flops | bytes accessed | tf_op | source)
XLA Modules:
  0.0 417.9 jit_solution(15163958304281575668)
XLA Ops:
  15.2 3.0 collective-permute-start.1
  18.3 5.4 %collective-permute-start.7 = (bf16[512,768]{1,0:T(8,128)(2,1)S(1)}, bf16[512,768]{1,0:T(8,128)(2,1)}, u32[]{:S(2)}, u32[]{:S(2)}) collective-permute-start(bf16[512,768]{1,0:T(8,128)(2,1)S(1)} %copy-done), channel_id=1, source_target_pairs={{0,2},{1,3},{2,4},{3,5},{4,6},{5,7},{8,10},{9,11},{10,12},{11,13},... | collective-permute-start | bytes 2359304 | tf_op jit(solution)/shard_map/ppermute | solution.py:697
  26.1 11.5 %collective-permute-done.1.refs_2_ = bf16[96,2432]{1,0:T(8,128)(2,1)} collective-permute-done((bf16[96,2432]{1,0:T(8,128)(2,1)}, bf16[96,2432]{1,0:T(8,128)(2,1)}, u32[]{:S(2)}, u32[]{:S(2)}) %collective-permute-start.1) | collective-permute-done | bytes 466976 | tf_op jit(solution)/shard_map/ppermute | solution.py:691
  37.6 3.5 collective-permute-start.3
  57.4 15.9 %collective-permute-done.3.refs_4_ = bf16[96,2432]{1,0:T(8,128)(2,1)} collective-permute-done((bf16[96,2432]{1,0:T(8,128)(2,1)}, bf16[96,2432]{1,0:T(8,128)(2,1)}, u32[]{:S(2)}, u32[]{:S(2)}) %collective-permute-start.3) | collective-permute-done | bytes 466976 | tf_op jit(solution)/shard_map/ppermute | solution.py:691
  73.3 12.5 %collective-permute-start.5 = (bf16[96,2432]{1,0:T(8,128)(2,1)}, bf16[96,2432]{1,0:T(8,128)(2,1)S(1)}, u32[]{:S(2)}, u32[]{:S(2)}) collective-permute-start(bf16[96,2432]{1,0:T(8,128)(2,1)} %collective-permute-done.3.refs_4_), channel_id=1, source_target_pairs={{0,2},{1,3},{2,6},{3,7},{4,0},{5,1},{6,4},{7,5},{8,10},{9,11},{10,... | collective-permute-start | bytes 1400840 | tf_op jit(solution)/shard_map/ppermute | solution.py:691
  85.7 4.3 %fusion.11 = (f32[1536,128]{1,0:T(8,128)}, f32[1536,128]{1,0:T(8,128)}) fusion(f32[128]{0:T(128)S(1)} %get-tuple-element.173, f32[128]{0:T(128)S(1)} %get-tuple-element.174, f32[1536]{0:T(1024)S(1)} %get-tuple-element.176), kind=kLoop, calls=%fused_computation.27 | loop fusion | flops 393216 | bytes 1580032 | tf_op jit(solution)/shard_map/mul | solution.py:73
  90.5 9.7 %collective-permute-done.5.refs_6_ = bf16[96,2432]{1,0:T(8,128)(2,1)S(1)} collective-permute-done((bf16[96,2432]{1,0:T(8,128)(2,1)}, bf16[96,2432]{1,0:T(8,128)(2,1)S(1)}, u32[]{:S(2)}, u32[]{:S(2)}) %collective-permute-start.5) | collective-permute-done | bytes 466976 | tf_op jit(solution)/shard_map/ppermute | solution.py:691
  104.0 12.9 %project.1 = (bf16[768,2432]{1,0:T(8,128)(2,1)}, bf16[1536,768]{1,0:T(8,128)(2,1)}, bf16[512,768]{1,0:T(8,128)(2,1)}, bf16[1536,768]{1,0:T(8,128)(2,1)}, bf16[1536,768]{1,0:T(8,128)(2,1)}) custom-call(s32[8]{0:T(128)} %stack.40.place, bf16[96,2432]{1,0:T(8,128)(2,1)} %concatenate.12.refs_0_, bf16[96,2432]{1,0:T(8,128)(2,1)} %collective-permute-done.refs_1_, ...), custom_call_target="tpu_custom_call" | custom-call | flops 3623878656 | bytes 20971520 | tf_op jit(solution)/shard_map/project/pallas_call | solution.py:131
  118.5 24.2 %attend.1 = (bf16[512,768]{1,0:T(8,128)(2,1)}, f32[6,8,512]{2,1,0:T(8,128)}) custom-call(bf16[512,768]{1,0:T(8,128)(2,1)} %get-tuple-element.40.q_ref, bf16[1536,768]{1,0:T(8,128)(2,1)} %get-tuple-element.41.k_ref, bf16[1536,768]{1,0:T(8,128)(2,1)} %get-tuple-element.42.v_ref, f32[2,1280,256]{2,1,0:T(8,128)} %pad_maximum_fusion.bias_ref), custom_call_target="tpu_custom_call" | custom-call | flops 8053063680 | bytes 10485760 | tf_op jit(solution)/shard_map/attend/pallas_call | solution.py:188
  142.7 6.8 %route.1 = (f32[512,768]{1,0:T(8,128)}, bf16[512,768]{1,0:T(8,128)(2,1)}, f32[512,128]{1,0:T(8,128)}, bf16[512,1536]{1,0:T(8,128)(2,1)}) custom-call(bf16[512,768]{1,0:T(8,128)(2,1)} %get-tuple-element.43.att_ref.o_ref, bf16[768,768]{1,0:T(8,128)(2,1)} %all-gather.8.cloned.1.call-done.col_ref, bf16[512,768]{1,0:T(8,128)(2,1)} %tok_ref.1, ...), custom_call_target="tpu_custom_call" | custom-call | flops 1811939328 | bytes 9437184 | tf_op jit(solution)/shard_map/route/pallas_call | solution.py:341
  149.5 25.3 %all_to_all.30 = bf16[4,128,1536]{2,1,0:T(8,128)(2,1)} all-to-all(bf16[4,128,1536]{2,1,0:T(8,128)(2,1)} %bitcast.72), channel_id=1, replica_groups=mesh['expert'=4,'fsdp'=8] {'expert'}, dimensions={0} | all-to-all | bytes 3145728 | tf_op jit(solution)/shard_map/all_to_all | solution.py:808
  174.8 3.4 all-gather.14.cloned.1.call-done
  178.3 15.7 %expert_rows.1 = (bf16[512,1536]{1,0:T(8,128)(2,1)}, bf16[3,512,2048]{2,1,0:T(8,128)(2,1)}) custom-call(bf16[512,1536]{1,0:T(8,128)(2,1)} %bitcast.70, bf16[768,2048]{1,0:T(8,128)(2,1)} %bitcast.81, bf16[768,2048]{1,0:T(8,128)(2,1)} %bitcast.82, bf16[768,2048]{1,0:T(8,128)(2,1)} %bitcast.83), custom_call_target="tpu_custom_call" | custom-call | flops 9663676416 | bytes 20971520 | tf_op jit(solution)/shard_map/expert_rows/pallas_call | solution.py:385
  194.0 20.2 %expert_sums.1 = bf16[768,6144]{1,0:T(8,128)(2,1)} custom-call(bf16[512,1536]{1,0:T(8,128)(2,1)} %bitcast.71, bf16[3,512,2048]{2,1,0:T(8,128)(2,1)} %get-tuple-element.65.low_ref), custom_call_target="tpu_custom_call" | custom-call | flops 4831838208 | bytes 20971520 | tf_op jit(solution)/shard_map/expert_sums/pallas_call | solution.py:422
  214.2 3.6 all-to-all-start.1
  219.4 18.3 %all-to-all-done.1 = bf16[4,128,1536]{2,1,0:T(8,128)(2,1)S(1)} async-done(((bf16[4,128,1536]{2,1,0:T(8,128)(2,1)}), bf16[4,128,1536]{2,1,0:T(8,128)(2,1)S(1)}, u32[]{:S(2)}, u32[]{:S(2)}) %all-to-all-start.1) | async-done | bytes 1572896 | tf_op jit(solution)/shard_map/all_to_all | solution.py:808
  238.8 14.0 %combine.1 = (bf16[512,768]{1,0:T(8,128)(2,1)}, f32[512,768]{1,0:T(8,128)}, bf16[512,768]{1,0:T(8,128)(2,1)}, f32[512,128]{1,0:T(8,128)}, bf16[768,768]{1,0:T(8,...) custom-call(bf16[512,1536]{1,0:T(8,128)(2,1)} %bitcast.68, f32[512,768]{1,0:T(8,128)} %get-tuple-element.47.residual_ref, ...), custom_call_target="tpu_custom_call" | custom-call | flops 2415919104 | bytes 14680064 | tf_op jit(solution)/shard_map/combine/pallas_call | solution.py:540
  252.9 25.4 %attend_back.1 = (bf16[512,768]{1,0:T(8,128)(2,1)}, bf16[1536,768]{1,0:T(8,128)(2,1)}, bf16[1536,768]{1,0:T(8,128)(2,1)}) custom-call(bf16[512,768]{1,0:T(8,128)(2,1)} %get-tuple-element.40.q_ref, bf16[1536,768]{1,0:T(8,128)(2,1)} %get-tuple-element.41.k_ref, bf16[1536,768]{1,0:T(8,128)(2,1)} %get-tuple-element.42.v_ref, ...), custom_call_target="tpu_custom_call" | custom-call | flops 20132659200 | bytes 20971520 | tf_op jit(solution)/shard_map/attend_back/pallas_call | solution.py:253
  278.3 10.8 %normed_grad.1 = (bf16[1024,768]{1,0:T(8,128)(2,1)}, f32[512,768]{1,0:T(8,128)}, f32[8,768]{1,0:T(8,128)}) custom-call(bf16[512,768]{1,0:T(8,128)(2,1)} %get-tuple-element.54.dq_ref, bf16[1536,768]{1,0:T(8,128)(2,1)} %get-tuple-element.55.dk_ref, bf16[1536,768]{1,0:T(8,128)(2,1)} %get-tuple-element.56.dv_ref, bf16[1536,768]{1,0:T(8,128)(2,1)} %copy-done.5, ...), custom_call_target="tpu_custom_call" | custom-call | flops 3623878656 | bytes 16777216 | tf_op jit(solution)/shard_map/normed_grad/pallas_call | solution.py:585
  289.1 11.9 %project_grad.1 = bf16[768,2560]{1,0:T(8,128)(2,1)} custom-call(bf16[1536,768]{1,0:T(8,128)(2,1)} %get-tuple-element.60.normed_ref, bf16[512,768]{1,0:T(8,128)(2,1)} %get-tuple-element.54.dq_ref, bf16[1536,768]{1,0:T(8,128)(2,1)} %get-tuple-element.55.dk_ref, bf16[1536,768]{1,0:T(8,128)(2,1)} %get-tuple-element.56.dv_ref, f32[8,768]{1,0:T(8,128)} %get-tuple-element.61.first_ref), custom_call_target="tpu_custom_call" | custom-call | flops 3623878656 | bytes 12582912 | tf_op jit(solution)/shard_map/project_grad/pallas_call | solution.py:648
  311.1 3.5 all-to-all-start.4
  317.0 8.1 %all-to-all-done.4 = bf16[4,96,896]{2,1,0:T(8,128)(2,1)S(1)} async-done(((bf16[4,96,896]{2,1,0:T(8,128)(2,1)}), bf16[4,96,896]{2,1,0:T(8,128)(2,1)S(1)}, u32[]{:S(2)}, u32[]{:S(2)}) %all-to-all-start.4) | async-done | bytes 688160 | tf_op jit(solution)/shard_map/all_to_all | solution.py:723
  326.0 3.4 all-to-all-start.5
  329.3 3.3 fusion
  332.6 3.6 all-to-all-done.5
  336.9 3.6 all-to-all-start.2
  348.0 18.4 %all_gather.23 = bf16[96,896]{1,0:T(8,128)(2,1)S(1)} all-gather(bf16[24,896]{1,0:T(8,128)(2,1)S(1)} %convert_element_type.130), channel_id=1, replica_groups=mesh['expert'=4,'fsdp'=8] {'expert'}, dimensions={0}, use_global_device_ids=true | all-gather | bytes 215040 | tf_op jit(solution)/shard_map/all_gather | solution.py:730
  381.2 4.1 all-to-all-start.3
  385.3 3.6 fusion.6
  388.9 7.7 %all-to-all-done.3 = bf16[4,24,2560]{2,1,0:T(8,128)(2,1)S(1)} async-done(((bf16[4,24,2560]{2,1,0:T(8,128)(2,1)}), bf16[4,24,2560]{2,1,0:T(8,128)(2,1)S(1)}, u32[]{:S(2)}, u32[]{:S(2)}) %all-to-all-start.3) | async-done | bytes 491552 | tf_op jit(solution)/shard_map/all_to_all | solution.py:726
  396.7 9.7 %all_gather.22 = bf16[96,2560]{1,0:T(8,128)(2,1)S(1)} all-gather(bf16[24,2560]{1,0:T(8,128)(2,1)S(1)} %reduce_sum.89), channel_id=1, replica_groups=mesh['expert'=4,'fsdp'=8] {'expert'}, dimensions={0}, use_global_device_ids=true | all-gather | bytes 614400 | tf_op jit(solution)/shard_map/all_gather | solution.py:730
  (147 shorter events, 69.3 us)
Async XLA Ops:
  7.2 11.1 %copy-start = (bf16[512,768]{1,0:T(8,128)(2,1)S(1)}, bf16[512,768]{1,0:T(8,128)(2,1)}, u32[]{:S(2)}) copy-start(bf16[512,768]{1,0:T(8,128)(2,1)} %tok_ref.1) | copy-start | bytes 2359300
  7.2 16.6 %copy-start.6 = (s32[512,2]{0,1:T(2,128)S(1)}, s32[512,2]{0,1:T(2,128)}, u32[]{:S(2)}) copy-start(s32[512,2]{0,1:T(2,128)} %param.20) | copy-start | bytes 12292
  7.2 135.5 %all-gather.8.cloned.1.call-start = ((), (), s32[]{:S(2)}) async-start(), calls=%async_computation.7 | async-start | bytes 1327104 | tf_op jit(solution)/shard_map/all_gather | solution.py:768
  7.9 166.9 %all-gather.10.cloned.1.call-start = ((), (), s32[]{:S(2)}) async-start(), calls=%async_computation.9 | async-start | bytes 3538944 | tf_op jit(solution)/shard_map/all_gather | solution.py:769
  8.7 15.5 %copy-start.14 = (s32[1,4]{1,0:T(1,128)S(1)}, s32[1,4]{1,0:T(1,128)}, u32[]{:S(2)}) copy-start(s32[1,4]{1,0:T(1,128)} %param.21) | copy-start | bytes 52
  8.7 166.1 %all-gather.12.cloned.1.call-start = ((), (), s32[]{:S(2)}) async-start(), calls=%async_computation.10 | async-start | bytes 3538944 | tf_op jit(solution)/shard_map/all_gather | solution.py:770
  9.4 168.8 %all-gather.14.cloned.1.call-start = ((), (), s32[]{:S(2)}) async-start(), calls=%async_computation.11 | async-start | bytes 3538944 | tf_op jit(solution)/shard_map/all_gather | solution.py:771
  15.2 22.3 %collective-permute-start.1 = (bf16[96,2432]{1,0:T(8,128)(2,1)}, bf16[96,2432]{1,0:T(8,128)(2,1)}, u32[]{:S(2)}, u32[]{:S(2)}) collective-permute-start(bf16[96,2432]{1,0:T(8,128)(2,1)} %concatenate.12.refs_0_), channel_id=1, source_target_pairs={{0,2},{1,3},{2,6},{3,7},{4,0},{5,1},{6,4},{7,5},{8,10},{9,11},{10,... | collective-permute-start | bytes 1400840 | tf_op jit(solution)/shard_map/ppermute | solution.py:691
  18.3 83.8 %collective-permute-start = (bf16[96,2432]{1,0:T(8,128)(2,1)}, bf16[96,2432]{1,0:T(8,128)(2,1)}, u32[]{:S(2)}, u32[]{:S(2)}) collective-permute-start(bf16[96,2432]{1,0:T(8,128)(2,1)} %concatenate.12.refs_0_), channel_id=1, source_target_pairs={{0,1},{1,0},{2,3},{3,2},{4,5},{5,4},{6,7},{7,6},{8,9},{9,8},{10,11... | collective-permute-start | bytes 1400840 | tf_op jit(solution)/shard_map/ppermute | solution.py:688
  18.3 37.6 %collective-permute-start.7 = (bf16[512,768]{1,0:T(8,128)(2,1)S(1)}, bf16[512,768]{1,0:T(8,128)(2,1)}, u32[]{:S(2)}, u32[]{:S(2)}) collective-permute-start(bf16[512,768]{1,0:T(8,128)(2,1)S(1)} %copy-done), channel_id=1, source_target_pairs={{0,2},{1,3},{2,4},{3,5},{4,6},{5,7},{8,10},{9,11},{10,12},{11,13},... | collective-permute-start | bytes 2359304 | tf_op jit(solution)/shard_map/ppermute | solution.py:697
  23.7 384.3 %reduce-scatter.2.cloned.1.call-start = ((), (), s32[]{:S(2)}) async-start(), calls=%async_computation.8 | async-start | bytes 10616832 | tf_op jit(solution)/shard_map/reduce_scatter | solution.py:815
  24.9 16.2 %copy-start.7 = (f32[512,8]{0,1:T(8,128)S(1)}, f32[512,8]{0,1:T(8,128)}, u32[]{:S(2)}) copy-start(f32[512,8]{0,1:T(8,128)} %param.19) | copy-start | bytes 49156
  24.9 16.2 %copy-start.8 = (f32[8,8]{1,0:T(8,128)S(1)}, f32[8,8]{1,0:T(8,128)}, u32[]{:S(2)}) copy-start(f32[8,8]{1,0:T(8,128)} %param.29) | copy-start | bytes 772
  25.6 16.7 %copy-start.9 = (s32[4]{0:T(128)S(1)}, s32[4]{0:T(128)}, u32[]{:S(2)}) copy-start(s32[4]{0:T(128)} %constant.160.clone) | copy-start | bytes 52
  37.6 35.7 %collective-permute-start.3 = (bf16[96,2432]{1,0:T(8,128)(2,1)}, bf16[96,2432]{1,0:T(8,128)(2,1)}, u32[]{:S(2)}, u32[]{:S(2)}) collective-permute-start(bf16[96,2432]{1,0:T(8,128)(2,1)} %collective-permute-done.1.refs_2_), channel_id=1, source_target_pairs={{0,2},{1,3},{2,6},{3,7},{4,0},{5,1},{6,4},{7,5},{8,10},{9,11},{10,... | collective-permute-start | bytes 1400840 | tf_op jit(solution)/shard_map/ppermute | solution.py:691
  57.3 44.7 %collective-permute-start.8 = (bf16[512,768]{1,0:T(8,128)(2,1)S(1)}, bf16[512,768]{1,0:T(8,128)(2,1)S(1)}, u32[]{:S(2)}, u32[]{:S(2)}) collective-permute-start(bf16[512,768]{1,0:T(8,128)(2,1)S(1)} %get-tuple-element.161), channel_id=1, source_target_pairs={{0,1},{1,0},{2,3},{3,2},{4,5},{5,4},{6,7},{7,6},{8,9},{9,8},{10,11... | collective-permute-start | bytes 2359304 | tf_op jit(solution)/shard_map/ppermute | solution.py:699
  73.3 27.0 %collective-permute-start.5 = (bf16[96,2432]{1,0:T(8,128)(2,1)}, bf16[96,2432]{1,0:T(8,128)(2,1)S(1)}, u32[]{:S(2)}, u32[]{:S(2)}) collective-permute-start(bf16[96,2432]{1,0:T(8,128)(2,1)} %collective-permute-done.3.refs_4_), channel_id=1, source_target_pairs={{0,2},{1,3},{2,6},{3,7},{4,0},{5,1},{6,4},{7,5},{8,10},{9,11},{10,... | collective-permute-start | bytes 1400840 | tf_op jit(solution)/shard_map/ppermute | solution.py:691
  90.0 12.1 %collective-permute-start.2 = (bf16[96,2432]{1,0:T(8,128)(2,1)}, bf16[96,2432]{1,0:T(8,128)(2,1)S(1)}, u32[]{:S(2)}, u32[]{:S(2)}) collective-permute-start(bf16[96,2432]{1,0:T(8,128)(2,1)} %collective-permute-done.1.refs_2_), channel_id=1, source_target_pairs={{0,1},{1,0},{2,3},{3,2},{4,5},{5,4},{6,7},{7,6},{8,9},{9,8},{10,11... | collective-permute-start | bytes 1400840 | tf_op jit(solution)/shard_map/ppermute | solution.py:688
  90.0 12.1 %collective-permute-start.4 = (bf16[96,2432]{1,0:T(8,128)(2,1)}, bf16[96,2432]{1,0:T(8,128)(2,1)S(1)}, u32[]{:S(2)}, u32[]{:S(2)}) collective-permute-start(bf16[96,2432]{1,0:T(8,128)(2,1)} %collective-permute-done.3.refs_4_), channel_id=1, source_target_pairs={{0,1},{1,0},{2,3},{3,2},{4,5},{5,4},{6,7},{7,6},{8,9},{9,8},{10,11... | collective-permute-start | bytes 1400840 | tf_op jit(solution)/shard_map/ppermute | solution.py:688
  100.3 1.7 copy-start.10
  100.3 1.9 collective-permute-start.6
  102.2 1.8 copy-start.13
  214.2 23.5 %all-to-all-start.1 = ((bf16[4,128,1536]{2,1,0:T(8,128)(2,1)}), bf16[4,128,1536]{2,1,0:T(8,128)(2,1)S(1)}, u32[]{:S(2)}, u32[]{:S(2)}) async-start(bf16[4,128,1536]{2,1,0:T(8,128)(2,1)} %bitcast.69), calls=%async_computation.1 | async-start | bytes 3145728 | tf_op jit(solution)/shard_map/all_to_all | solution.py:808
  304.9 24.4 %collective-permute-start.11 = (bf16[4,4,24,2560]{3,2,0,1:T(8,128)(2,1)}, bf16[4,4,24,2560]{3,2,0,1:T(8,128)(2,1)}, u32[]{:S(2)}, u32[]{:S(2)}) collective-permute-start(bf16[4,4,24,2560]{3,2,0,1:T(8,128)(2,1)} %bitcast.59), channel_id=1, source_target_pairs={{0,1},{1,0},{2,3},{3,2},{4,5},{5,4},{6,7},{7,6},{8,9},{9,8},{10,11... | collective-permute-start | bytes 5898248 | tf_op jit(solution)/shard_map/ppermute | solution.py:720
  307.7 2.4 collective-permute-start.12
  311.1 14.0 %all-to-all-start.4 = ((bf16[4,96,896]{2,1,0:T(8,128)(2,1)}), bf16[4,96,896]{2,1,0:T(8,128)(2,1)S(1)}, u32[]{:S(2)}, u32[]{:S(2)}) async-start(bf16[4,96,896]{2,1,0:T(8,128)(2,1)} %bitcast.65), calls=%async_computation.4 | async-start | bytes 1376256 | tf_op jit(solution)/shard_map/all_to_all | solution.py:723
  316.7 23.9 %collective-permute-start.9 = (bf16[512,768]{1,0:T(8,128)(2,1)}, bf16[512,768]{1,0:T(8,128)(2,1)S(1)}, u32[]{:S(2)}, u32[]{:S(2)}) collective-permute-start(bf16[512,768]{1,0:T(8,128)(2,1)} %slice.75), channel_id=1, source_target_pairs={{0,1},{1,0},{2,3},{3,2},{4,5},{5,4},{6,7},{7,6},{8,9},{9,8},{10,11... | collective-permute-start | bytes 2359304 | tf_op jit(solution)/shard_map/ppermute | solution.py:706
  326.0 10.3 %all-to-all-start.5 = ((bf16[4,24,896]{2,1,0:T(8,128)(2,1)}), bf16[4,24,896]{2,1,0:T(8,128)(2,1)S(1)}, u32[]{:S(2)}, u32[]{:S(2)}) async-start(bf16[4,24,896]{2,1,0:T(8,128)(2,1)} %bitcast.76), calls=%async_computation.5 | async-start | bytes 344064 | tf_op jit(solution)/shard_map/all_to_all | solution.py:726
  336.9 43.1 %all-to-all-start.2 = ((bf16[4,96,2560]{2,1,0:T(8,128)(2,1)}), bf16[4,96,2560]{2,1,0:T(8,128)(2,1)S(1)}, u32[]{:S(2)}, u32[]{:S(2)}) async-start(bf16[4,96,2560]{2,1,0:T(8,128)(2,1)} %bitcast.29), calls=%async_computation.2 | async-start | bytes 3932160 | tf_op jit(solution)/shard_map/all_to_all | solution.py:723
  342.8 35.0 %copy-start.1 = (bf16[512,768]{1,0:T(8,128)(2,1)S(1)}, bf16[512,768]{1,0:T(8,128)(2,1)}, u32[]{:S(2)}) copy-start(bf16[512,768]{1,0:T(8,128)(2,1)} %tok_ref.1) | copy-start | bytes 2359300
  342.8 35.0 %collective-permute-start.10 = (bf16[512,768]{1,0:T(8,128)(2,1)}, bf16[512,768]{1,0:T(8,128)(2,1)}, u32[]{:S(2)}, u32[]{:S(2)}) collective-permute-start(bf16[512,768]{1,0:T(8,128)(2,1)} %fusion.8), channel_id=1, source_target_pairs={{2,0},{3,1},{4,2},{5,3},{6,4},{7,5},{10,8},{11,9},{12,10},{13,11},... | collective-permute-start | bytes 2359304 | tf_op jit(solution)/shard_map/ppermute | solution.py:708
  381.2 15.4 %all-to-all-start.3 = ((bf16[4,24,2560]{2,1,0:T(8,128)(2,1)}), bf16[4,24,2560]{2,1,0:T(8,128)(2,1)S(1)}, u32[]{:S(2)}, u32[]{:S(2)}) async-start(bf16[4,24,2560]{2,1,0:T(8,128)(2,1)} %bitcast.66), calls=%async_computation.3 | async-start | bytes 983040 | tf_op jit(solution)/shard_map/all_to_all | solution.py:726
  (6 other events, 7.8 us)
Sparse Core Ops, SparseCore 0:
  9.7 35.3 all-gather.7
  46.7 51.3 all-gather.9
  99.7 39.8 all-gather.11
  141.1 37.1 all-gather.13
  214.4 98.3 reduce-scatter.1
